TPU v7x, 32 devices: a whole 2x2x4 slice. The times are simulated.
32 devices in a mesh: seq: 4 (over y, core), dp: 8 (over z, x).
Axes of the slice: x: 2, y: 2, z: 4, core: 2. Of those that a mesh axis runs over, the one named last changes fastest.
Arguments:
- tokens: bfloat16 [8, 768, 768], P('dp', 'seq'), may hold values from -6 to 6
- lengths: int32 [8], P('dp'), may hold values from 192 to 768, as said below
- norm_one: bfloat16 [768], P(('seq', 'dp')), may hold values from 0.099609375 to 1.8984375
- query_one: bfloat16 [768, 768], P(('seq', 'dp')), may hold values from -0.21875 to 0.21875
- key_one: bfloat16 [768, 768], P(('seq', 'dp')), may hold values from -0.21875 to 0.21875
- value_one: bfloat16 [768, 768], P(('seq', 'dp')), may hold values from -0.21875 to 0.21875
- shift_taps: bfloat16 [768, 64], P(('seq', 'dp')), may hold values from -0.75 to 0.75
- decay_log: bfloat16 [768, 64], P(('seq', 'dp')), may hold values from -9 to -1.1953125
- turn_angle: bfloat16 [768, 64], P(('seq', 'dp')), may hold values from -3.140625 to 3.140625
- mix_real: bfloat16 [768, 64], P(('seq', 'dp')), may hold values from -0.059814453 to 0.059814453
- mix_imag: bfloat16 [768, 64], P(('seq', 'dp')), may hold values from -0.059814453 to 0.059814453
- skip_gain: bfloat16 [768], P(('seq', 'dp')), may hold values from -4 to 4
- out_one: bfloat16 [768, 768], P(('seq', 'dp')), may hold values from -0.21875 to 0.21875
- norm_two: bfloat16 [768], P(('seq', 'dp')), may hold values from 0.099609375 to 1.8984375
- up_one: bfloat16 [768, 3072], P(('seq', 'dp')), may hold values from -0.21875 to 0.21875
- down_one: bfloat16 [3072, 768], P(('seq', 'dp')), may hold values from -0.109375 to 0.109375
- norm_three: bfloat16 [768], P(('seq', 'dp')), may hold values from 0.099609375 to 1.8984375
- qkv_weight: bfloat16 [768, 2304], P(('seq', 'dp')), may hold values from -0.21875 to 0.21875
- out_two: bfloat16 [768, 768], P(('seq', 'dp')), may hold values from -3 to 3
- norm_four: bfloat16 [768], P(('seq', 'dp')), may hold values from 0.099609375 to 1.8984375
- up_two: bfloat16 [768, 3072], P(('seq', 'dp')), may hold values from -0.21875 to 0.21875
- down_two: bfloat16 [3072, 768], P(('seq', 'dp')), may hold values from -0.109375 to 0.109375
- cotangent: bfloat16 [8, 768, 768], P('dp', 'seq'), may hold values from -6 to 6
Outputs:
- activations: bfloat16 [8, 768, 768], P('dp', 'seq')
- input_grad: float32 [8, 768, 768], P('dp', 'seq')
- grad_norm_one: float32 [768], P(('seq', 'dp'))
- grad_query_one: float32 [768, 768], P(('seq', 'dp'))
- grad_key_one: float32 [768, 768], P(('seq', 'dp'))
- grad_value_one: float32 [768, 768], P(('seq', 'dp'))
- grad_shift_taps: float32 [768, 64], P(('seq', 'dp'))
- grad_decay_log: float32 [768, 64], P(('seq', 'dp'))
- grad_turn_angle: float32 [768, 64], P(('seq', 'dp'))
- grad_mix_real: float32 [768, 64], P(('seq', 'dp'))
- grad_mix_imag: float32 [768, 64], P(('seq', 'dp'))
- grad_skip_gain: float32 [768], P(('seq', 'dp'))
- grad_out_one: float32 [768, 768], P(('seq', 'dp'))
- grad_norm_two: float32 [768], P(('seq', 'dp'))
- grad_up_one: float32 [768, 3072], P(('seq', 'dp'))
- grad_down_one: float32 [3072, 768], P(('seq', 'dp'))
- grad_norm_three: float32 [768], P(('seq', 'dp'))
- grad_qkv_weight: float32 [768, 2304], P(('seq', 'dp'))
- grad_out_two: float32 [768, 768], P(('seq', 'dp'))
- grad_norm_four: float32 [768], P(('seq', 'dp'))
- grad_up_two: float32 [768, 3072], P(('seq', 'dp'))
- grad_down_two: float32 [3072, 768], P(('seq', 'dp'))
Inputs may be any that keep to these rules, and one draw needn't show every extreme that they name: `lengths`: in each aligned run of four sequences exactly one, which one drawn from the seed, has 192 tokens and the other three have 768.
All inputs are finite; a program needn't handle non-finite values.
Results may differ from a plain program's by a relative error of at most 0.024.
Values may be sent and summed in bfloat16 or wider, within the bound.
A program may use at most 320 MiB of HBM per device.

v0:
```python
from functools import partial

import jax
import jax.numpy as jnp
from jax import lax
from jax.experimental import pallas as pl
from jax.experimental.pallas import tpu as pltpu
from jax.sharding import PartitionSpec as P

HEADS = 12
HDIM = 64
EPSILON = 1e-05
HIGHEST = lax.Precision.HIGHEST
MASKED = -1e30
BOTH = ("seq", "dp")
MESH = pl.DeviceIdType.MESH
MIB = 1024 * 1024
LAGS = (0, 2, 4, 6)
PLACES = (4, 5, 6, 7, 9)
MIDDLE = (1, 1, 2, 3, 4, 5, 6, 7, 8)
EARLY = 2
RUNS = (8, 11, 12, 14, 15, 17)
AHEAD = 4
F32 = jnp.float32
BF16 = jnp.bfloat16


def grouped():
    return lax.axis_size("seq") == 4 and lax.axis_size("dp") == 8


def coordinates():
    seq, dp = lax.axis_index("seq"), lax.axis_index("dp")
    return seq // 2, seq % 2, dp // 2, dp % 2


def slot_of(y, c, z, x):
    return (y * 2 + c) * 8 + z * 2 + x


def device_of(y, c, z, x):
    return (y * 2 + c, z * 2 + x)


def greet(peers):
    barrier = pltpu.get_barrier_semaphore()
    for peer in peers:
        pl.semaphore_signal(barrier, inc=1, device_id=peer, device_id_type=MESH)
    pl.semaphore_wait(barrier, len(peers))


def six_peers(y, c, z, x):
    return [device_of(y, c, (z + k) % 4, x) for k in (1, 2, 3)] + [
        device_of(y, c, z, 1 - x),
        device_of(1 - y, c, z, x),
        device_of(y, 1 - c, z, x),
    ]


class Gather:
    def __init__(self, parts, sources, gathered, local_sem, send_sem, recv_sem, ahead=None):
        self.parts, self.sources, self.gathered = parts, sources, gathered
        self.send_sem, self.recv_sem, self.ahead = send_sem, recv_sem, ahead or AHEAD
        self.y, self.c, self.z, self.x = y, c, z, x = coordinates()
        self.me = slot_of(y, c, z, x)
        self.across_x = device_of(y, c, z, 1 - x)
        self.across_y = device_of(1 - y, c, z, x)
        self.other_core = device_of(y, 1 - c, z, x)
        self.own = [
            pltpu.make_async_copy(sources[i], gathered[i].at[self.me], local_sem.at[i])
            for i in range(len(sources))
        ]
        self.done = 0

    def place(self, p, slot):
        i, row, rows, column, columns, _ = self.parts[p]
        return self.gathered[i].at[slot, pl.ds(row, rows), pl.ds(column, columns)]

    def send(self, p, slot, target, first=False):
        i, row, rows, column, columns, _ = self.parts[p]
        source = self.sources[i].at[pl.ds(row, rows), pl.ds(column, columns)]
        pltpu.make_async_remote_copy(
            src_ref=source if first else self.place(p, slot),
            dst_ref=self.place(p, slot),
            send_sem=self.send_sem.at[p],
            recv_sem=self.recv_sem.at[p, slot],
            device_id=target,
            device_id_type=MESH,
        ).start()

    def arrived(self, p, slot):
        place = self.place(p, slot)
        pltpu.make_async_copy(place, place, self.recv_sem.at[p, slot]).wait()

    def first(self, p):
        for k in (1, 3, 2):
            self.send(p, self.me, device_of(self.y, self.c, (self.z + k) % 4, self.x), True)
        self.send(p, self.me, self.across_x, True)
        self.send(p, self.me, self.across_y, True)
        self.send(p, self.me, self.other_core, True)

    def start(self):
        for copy in self.own:
            copy.start()
        for p in range(min(self.ahead, len(self.parts))):
            self.first(p)

    def after_z(self, p):
        for k in (3, 1, 2):
            slot = slot_of(self.y, self.c, (self.z + k) % 4, self.x)
            self.arrived(p, slot)
            self.send(p, slot, self.across_x)
            self.send(p, slot, self.across_y)
            self.send(p, slot, self.other_core)

    def after_first(self, p):
        x_first = self.parts[p][5]
        for k in (0, 3, 1, 2):
            by_x = slot_of(self.y, self.c, (self.z + k) % 4, 1 - self.x)
            by_y = slot_of(1 - self.y, self.c, (self.z + k) % 4, self.x)
            self.arrived(p, by_x)
            if x_first:
                self.send(p, by_x, self.across_y)
            self.send(p, by_x, self.other_core)
            self.arrived(p, by_y)
            if not x_first:
                self.send(p, by_y, self.across_x)
            self.send(p, by_y, self.other_core)

    def after_second(self, p):
        for k in (0, 3, 1, 2):
            slot = slot_of(1 - self.y, self.c, (self.z + k) % 4, 1 - self.x)
            self.arrived(p, slot)
            self.send(p, slot, self.other_core)

    def whole(self, p):
        for side in (0, 1):
            for zz in range(4):
                for xx in (0, 1):
                    self.arrived(p, slot_of(side, 1 - self.c, zz, xx))

    def steps(self):
        return len(self.parts) + 3

    def run(self, until):
        while self.done < min(until, self.steps()):
            s, count = self.done, len(self.parts)
            if self.ahead <= s + self.ahead < count:
                self.first(s + self.ahead)
            for stage, act in enumerate(
                (self.after_z, self.after_first, self.after_second, self.whole)
            ):
                if 0 <= s - stage < count:
                    act(s - stage)
            self.done += 1

    def own_arrived(self, indices):
        for i in indices:
            self.own[i].wait()

    def finish(self):
        self.run(self.steps())
        for p, (i, row, rows, column, columns, _) in enumerate(self.parts):
            sent = self.gathered[i].at[pl.ds(0, 31), pl.ds(row, rows), pl.ds(column, columns)]
            pltpu.make_async_copy(sent, sent, self.send_sem.at[p]).wait()


def cut(arrays):
    parts = []
    for i, (rows, columns) in enumerate(arrays):
        if columns > 1536:
            width = 1536 if columns % 1536 == 0 else 768
            pieces = [(0, rows, w, width) for w in range(0, columns, width)]
        elif rows > 48:
            pieces = [(r, 48, 0, columns) for r in range(0, rows, 48)]
        else:
            pieces = [(0, rows, 0, columns)]
        for piece in pieces:
            parts.append((i,) + piece + (len(parts) % 2 == 0,))
    return parts


class Reduce:
    def __init__(self, parts, terms, totals, buffers, mine, send_sem, recv_sem, mine_sem):
        self.parts, self.terms, self.totals, self.buffers = parts, terms, totals, buffers
        self.send_sem, self.recv_sem, self.mine_sem = send_sem, recv_sem, mine_sem
        self.y, self.c, self.z, self.x = coordinates()
        self.mine, self.kinds = mine, {}
        for p, part in enumerate(parts):
            if part[0] < len(mine[0]):
                self.kinds.setdefault((part[2], part[4]), []).append(p)
        self.done = 0

    def term(self, p, core):
        i, row, rows, column, columns, _ = self.parts[p]
        return self.terms[i].at[:, core, :, :, pl.ds(row, rows), pl.ds(column, columns)]

    def fetch(self, p):
        kind = (self.parts[p][2], self.parts[p][4])
        place = self.kinds[kind].index(p)
        held = self.mine[1][kind].at[place % 2]
        return pltpu.make_async_copy(self.term(p, self.c), held, self.mine_sem.at[p]), held

    def copies(self, p, stage):
        one, two, three, four = self.buffers[4 * p : 4 * p + 4]
        y, c, z, x = self.y, self.c, self.z, self.x
        across_x, across_y = device_of(y, c, z, 1 - x), device_of(1 - y, c, z, x)
        x_last = self.parts[p][5]
        if stage == 0:
            pairs = [(self.term(p, 1 - c), one, device_of(y, 1 - c, z, x))]
        elif stage == 1 and x_last:
            pairs = [(one.at[1 - y], two, across_y)]
        elif stage == 1:
            pairs = [(one.at[:, :, 1 - x], two, across_x)]
        elif stage == 2 and x_last:
            pairs = [(two.at[:, 1 - x], three, across_x)]
        elif stage == 2:
            pairs = [(two.at[1 - y], three, across_y)]
        else:
            pairs = [
                (three.at[(z + k) % 4], four.at[k - 1], device_of(y, c, (z + k) % 4, x))
                for k in (1, 2, 3)
            ]
        return [
            pltpu.make_async_remote_copy(
                src_ref=src,
                dst_ref=dst,
                send_sem=self.send_sem.at[p, stage + n],
                recv_sem=self.recv_sem.at[p, stage + n],
                device_id=target,
                device_id_type=MESH,
            )
            for n, (src, dst, target) in enumerate(pairs)
        ]

    def add(self, p, stage):
        one, two, three, four = self.buffers[4 * p : 4 * p + 4]
        y, c, z, x = self.y, self.c, self.z, self.x
        i, row, rows, column, columns, x_last = self.parts[p]

        def total(a, b):
            return (a.astype(F32) + b.astype(F32)).astype(a.dtype)

        if stage == 0:
            if i < len(self.mine[0]):
                copy, held = self.fetch(p)
                copy.wait()
            else:
                held = self.term(p, c)

            def add_one(k, _):
                b, zz = k // 4, k % 4
                for xx in (0, 1):
                    one[b, zz, xx] = total(one[b, zz, xx], held[b, zz, xx])
                return 0

            lax.fori_loop(0, 8, add_one, 0)
            if i < len(self.mine[0]):
                same = self.kinds[(rows, columns)]
                later = same.index(p) + 2
                if later < len(same):
                    self.fetch(same[later])[0].start()
        elif stage == 1:

            def add_two(k, _):
                for h in (0, 1):
                    if x_last:
                        two[k, h] = total(two[k, h], one[y, k, h])
                    else:
                        two[h, k] = total(two[h, k], one[h, k, x])
                return 0

            lax.fori_loop(0, 4, add_two, 0)
        elif stage == 2:

            def add_three(k, _):
                three[k] = total(three[k], two[k, x] if x_last else two[y, k])
                return 0

            lax.fori_loop(0, 4, add_three, 0)
        else:
            self.totals[i][pl.ds(row, rows), pl.ds(column, columns)] = (
                three[z].astype(F32)
                + four[0].astype(F32)
                + four[1].astype(F32)
                + four[2].astype(F32)
            )

    def start(self, arrays):
        for p, part in enumerate(self.parts):
            if part[0] in arrays:
                for copy in self.copies(p, 0):
                    copy.start()

    def fetch_first(self):
        for same in self.kinds.values():
            for p in same[:2]:
                self.fetch(p)[0].start()

    def steps(self):
        return len(self.parts) + LAGS[3]

    def run(self, until):
        while self.done < min(until, self.steps()):
            for stage in range(4):
                p = self.done - LAGS[stage]
                if 0 <= p < len(self.parts):
                    for copy in self.copies(p, stage):
                        copy.wait_recv()
                    self.add(p, stage)
                    if stage < 3:
                        for copy in self.copies(p, stage + 1):
                            copy.start()
            self.done += 1

    def finish(self):
        self.run(self.steps())
        for p in range(len(self.parts)):
            for stage in range(4):
                for copy in self.copies(p, stage):
                    copy.wait_send()


def all_others():
    rows, groups = lax.axis_size("seq"), lax.axis_size("dp")
    count = rows * groups
    me = lax.axis_index("seq") * groups + lax.axis_index("dp")
    others = [lax.rem(me + k, count) for k in range(1, count)]
    return me, others, [(o // groups, lax.rem(o, groups)) for o in others]


class Swap:
    def __init__(self, src, dst, send_sem, recv_sem):
        self.src, self.dst, self.send_sem, self.recv_sem = src, dst, send_sem, recv_sem

    def start(self):
        me, others, places = all_others()
        for o, place in zip(others, places):
            pltpu.make_async_remote_copy(
                src_ref=self.src.at[o],
                dst_ref=self.dst.at[me],
                send_sem=self.send_sem,
                recv_sem=self.recv_sem,
                device_id=place,
                device_id_type=MESH,
            ).start()

    def wait(self):
        most = pl.ds(0, self.src.shape[0] - 1)
        me = all_others()[0]
        pltpu.make_async_copy(self.src.at[most], self.dst.at[most], self.recv_sem).wait()
        pltpu.make_async_copy(self.src.at[most], self.dst.at[most], self.send_sem).wait()
        self.dst[me] = self.src[me]


def layer_norm(residual, scale_gain):
    average = jnp.mean(residual, axis=-1, keepdims=True)
    centered = residual - average
    variance = jnp.mean(centered * centered, axis=-1, keepdims=True)
    return centered * lax.rsqrt(variance + EPSILON) * scale_gain


def contract(left_side, right_side, left_dim, right_dim):
    return lax.dot_general(
        left_side,
        right_side,
        (((left_dim,), (right_dim,)), ((), ())),
        preferred_element_type=F32,
    )


def product(left_side, right_side):
    return contract(left_side, right_side, 1, 0)


def product_back(left_side, right_side):
    return contract(left_side, right_side, 1, 1)


def product_sum(left_side, right_side):
    return contract(left_side, right_side, 0, 0)


def feed_forward(residual, scale_gain, up_weight, down_weight):
    normed = layer_norm(residual, scale_gain).astype(BF16)
    pre_act = product(normed, up_weight)
    activated = jax.nn.gelu(pre_act).astype(BF16)
    return (residual + product(activated, down_weight), (normed, pre_act, activated))


def feed_back(residual, scale_gain, up_weight, down_weight, stored, grad_residual):
    normed, pre_act, activated = stored
    grad_branch = grad_residual.astype(BF16)
    grad_down = product_sum(activated, grad_branch)
    grad_activated = product_back(grad_branch, down_weight)
    gelu_pull = jax.vjp(jax.nn.gelu, pre_act)[1]
    grad_pre = gelu_pull(grad_activated)[0].astype(BF16)
    grad_up = product_sum(normed, grad_pre)
    grad_normed = product_back(grad_pre, up_weight)
    norm_pull = jax.vjp(layer_norm, residual, scale_gain)[1]
    grad_input, grad_gain = norm_pull(grad_normed)
    return (grad_residual + grad_input, grad_gain, grad_up, grad_down)


def ssm_kernel(decay_log, turn_angle, mix_real, mix_imag, length):
    rate = jnp.exp(decay_log)[:, :, None]
    angle = turn_angle[:, :, None]
    step = 32

    def powers(times):
        return (
            jnp.exp(-times * rate) * jnp.cos(times * angle),
            jnp.exp(-times * rate) * jnp.sin(times * angle),
        )

    low_real, low_imag = powers(jnp.arange(step, dtype=F32)[None, None])
    high_real, high_imag = powers(
        (step * jnp.arange(length // step, dtype=jnp.int32)).astype(F32)[None, None]
    )
    real, imag = mix_real[:, :, None], mix_imag[:, :, None]
    high = jnp.concatenate(
        [real * high_real - imag * high_imag, -(real * high_imag + imag * high_real)], axis=1
    )
    low = jnp.concatenate([low_real, low_imag], axis=1)
    kernel = jnp.einsum("cna,cnb->cab", high, low, precision=HIGHEST)
    return kernel.reshape(decay_log.shape[0], length)


def state_columns(decay, turn, real, imag, cols):
    states = decay.shape[1]
    size = jnp.exp(-jnp.exp(decay))
    turned = [a.T for a in (size * jnp.cos(turn), size * jnp.sin(turn), real, imag)]
    for ch in range(decay.shape[0]):
        for n, a in enumerate(turned):
            cols[ch * states : (ch + 1) * states, n : n + 1] = a[:, ch : ch + 1]


def state_powers(cols, ch, states):
    own = cols[pl.ds(pl.multiple_of(ch * states, states), states), :]
    base_real, base_imag = own[:, :1], own[:, 1:2]
    lane = lax.broadcasted_iota(jnp.int32, (states, 128), 1)
    real, imag = jnp.ones((states, 128), F32), jnp.zeros((states, 128), F32)
    for bit in range(7):
        taken = lane % (2 << bit) >= (1 << bit)
        step_real = jnp.where(taken, base_real, 1.0)
        step_imag = jnp.where(taken, base_imag, 0.0)
        real, imag = real * step_real - imag * step_imag, real * step_imag + imag * step_real
        base_real, base_imag = (
            base_real * base_real - base_imag * base_imag, 2.0 * base_real * base_imag
        )
    return real, imag, base_real, base_imag, own[:, 2:3], own[:, 3:4]


def kernel_rows(decay, turn, real_mix, imag_mix, cols, kernel_ref, length):
    states = decay.shape[1]
    state_columns(decay, turn, real_mix, imag_mix, cols)
    kernel_ref[...] = jnp.zeros_like(kernel_ref)

    def one(ch, _):
        real, imag, jump_real, jump_imag, mix_real, mix_imag = state_powers(cols, ch, states)
        for first in range(0, length, 128):
            terms = mix_real * real - mix_imag * imag
            kernel_ref[ch, :, first : first + 128] = jnp.sum(terms, axis=0, keepdims=True)
            real, imag = (
                real * jump_real - imag * jump_imag, real * jump_imag + imag * jump_real
            )
        return 0

    lax.fori_loop(0, decay.shape[0], one, 0)


def kernel_rows_back(decay, turn, real_mix, imag_mix, cols, sums, grad_ref, length):
    channels, states = decay.shape
    state_columns(decay, turn, real_mix, imag_mix, cols)
    lane = lax.broadcasted_iota(jnp.int32, (states, 128), 1)

    def one(ch, _):
        real, imag, jump_real, jump_imag, _, _ = state_powers(cols, ch, states)
        totals = [jnp.zeros((states, 128), F32)] * 4
        for first in range(0, length, 128):
            grad = grad_ref[ch, :, first : first + 128]
            times = (first + lax.broadcasted_iota(jnp.int32, (1, 128), 1)).astype(F32)
            parts = (grad * real, grad * imag, grad * times * real, grad * times * imag)
            totals = [a + b for a, b in zip(totals, parts)]
            real, imag = (
                real * jump_real - imag * jump_imag, real * jump_imag + imag * jump_real
            )
        kept = jnp.zeros((states, 128), F32)
        for n, a in enumerate(totals):
            kept = jnp.where(lane == n, jnp.sum(a, axis=1, keepdims=True), kept)
        sums[pl.ds(pl.multiple_of(ch * states, states), states), :] = kept
        return 0

    lax.fori_loop(0, channels, one, 0)
    plain_real, plain_imag, timed_real, timed_imag = [
        jnp.concatenate(
            [sums[ch * states : (ch + 1) * states, n : n + 1] for ch in range(channels)], axis=1
        ).T
        for n in range(4)
    ]
    return (
        -jnp.exp(decay) * (real_mix * timed_real - imag_mix * timed_imag),
        -(real_mix * timed_imag + imag_mix * timed_real),
        plain_real,
        -plain_imag,
    )


def toeplitz(row, rows):
    spread = jnp.broadcast_to(row, (rows, row.shape[1]))
    return pltpu.roll(spread, 0, 1, stride=1, stride_axis=0)


def block_sum(mixed, blocks, groups, rows):
    total = mixed[:, :rows]
    for d in range(1, blocks):
        piece = mixed[: (blocks - d) * groups, d * rows : (d + 1) * rows]
        total = total + jnp.concatenate(
            [jnp.zeros((d * groups, rows), piece.dtype), piece], axis=0
        )
    return total


def block_spread(value, blocks, lags, groups, rows):
    pieces = [value]
    for d in range(1, lags):
        pieces.append(
            jnp.concatenate(
                [value[d * groups :], jnp.zeros((d * groups, rows), value.dtype)], axis=0
            )
        )
    return jnp.concatenate(pieces, axis=1)


def mix(blocks, groups, rows, keys, values, tap_row, kernel_row, skip):
    span = blocks * rows
    taps = toeplitz(tap_row, rows)[:, : 2 * rows].astype(BF16)
    longer = toeplitz(kernel_row, rows)[:, :span].astype(BF16)
    near = product(keys, taps)
    shifted = near[:, :rows] + jnp.concatenate(
        [jnp.zeros((groups, rows), F32), near[: (blocks - 1) * groups, rows:]], axis=0
    )
    signal = shifted * values.astype(F32)
    mixed = product(signal.astype(BF16), longer)
    return shifted, block_sum(mixed, blocks, groups, rows) + skip * signal


def mixer_body(blocks, groups, rows, k_ref, v_ref, taps_ref, kernel_ref, skip_ref, shifted_ref, out_ref):
    for ch in range(k_ref.shape[0]):
        row = slice(ch, ch + 1)
        shifted_ref[ch], out = mix(
            blocks, groups, rows, k_ref[ch], v_ref[ch],
            taps_ref[row, :], kernel_ref[row, :], skip_ref[row, :1],
        )
        out_ref[ch] = out.astype(BF16)


def flat_weight(ref):
    wide = ref[...].astype(F32)
    return wide.reshape(wide.shape[0] * wide.shape[1], wide.shape[2]).astype(BF16)


def flat_part(ref, first, width):
    wide = ref[:, :, first : first + width].astype(F32)
    return wide.reshape(wide.shape[0] * wide.shape[1], width).astype(BF16)


def first_body(parts, count, *refs):
    sources = refs[:count]
    tokens, live, key_live, small, taps = refs[count : count + 5]
    states = refs[count + 5 : count + 9]
    refs = refs[count + 9 :]
    gathered = refs[:count]
    (
        residual_ref, standard_ref, inverse_ref, normed_ref, queries_ref, ssm_ref, gated_ref,
        k_ref, v_ref, shifted_ref,
        normed_two, pre_one, act_one, residual_two, normed_three, att_q, att_kv, attended,
        log_total, residual_three, taps_ref, kernel_ref,
    ) = refs[count : count + 22]
    (
        wide, sent_kv, came_kv, sent_y, came_y, up, down, qkv, out_two, cols,
        local_sem, send_sem, recv_sem, swap_sem, load_sem, line_send, line_recv,
    ) = refs[count + 22 :]
    gains, key_all, value_all, query_all, out_all = gathered[:5]
    devices, channels = key_all.shape[0], key_all.shape[1]
    rows, features = tokens.shape
    blocks, groups = lax.axis_size("seq"), lax.axis_size("dp")
    greet(all_others()[2])
    gather = Gather(parts, sources, gathered, local_sem, send_sem, recv_sem)
    gather.start()

    turned = tokens[...].astype(F32).T
    centered = turned - jnp.mean(turned, axis=0, keepdims=True)
    inverse = lax.rsqrt(jnp.mean(centered * centered, axis=0, keepdims=True) + EPSILON)
    inverse_ref[...] = jnp.broadcast_to(inverse, inverse_ref.shape)
    standard_ref[...] = centered * inverse
    tap_count = taps.shape[1]
    taps_ref[...] = jnp.zeros_like(taps_ref)
    taps_ref[:, :tap_count] = taps[...].astype(F32)
    gather.run(EARLY)
    kernel_rows(*[a[...].astype(F32) for a in states], cols, kernel_ref, blocks * rows)
    gather.run(RUNS[0])
    gather.own_arrived(range(5))
    all_gains = gains[...].reshape(features, 128)
    normed_ref[...] = (standard_ref[...] * all_gains[:, :1]).astype(BF16)

    def projected(weight):
        return contract(flat_weight(weight), normed_ref[...], 0, 0)

    wide[:, :channels, :] = projected(key_all).reshape(devices, channels, rows)
    wide[:, channels:, :] = (projected(value_all) * live[...]).reshape(devices, channels, rows)
    sent_kv[...] = wide[...].astype(BF16)
    over = Swap(sent_kv, came_kv, swap_sem.at[0], swap_sem.at[1])
    over.start()
    queries_ref[...] = projected(query_all)
    gather.run(RUNS[1])
    over.wait()
    wide[...] = came_kv[...].astype(F32)
    for ch in range(channels):
        row = slice(ch, ch + 1)
        k_ref[ch] = wide[:, ch, :].astype(BF16)
        v_ref[ch] = wide[:, channels + ch, :].astype(BF16)
        shifted_ref[ch], out = mix(
            blocks, groups, rows, k_ref[ch], v_ref[ch],
            taps_ref[row, :], kernel_ref[ch], small[row, 4:5],
        )
        wide[:, ch, :] = out
        if ch == channels // 2:
            gather.run(RUNS[2])
    sent_y[...] = wide[:, :channels, :].astype(BF16)
    back = Swap(sent_y, came_y, swap_sem.at[2], swap_sem.at[3])
    back.start()
    gather.run(RUNS[3])
    gather.own_arrived(range(5, count))
    loads = [
        pltpu.make_async_copy(gathered[5 + n], held, load_sem.at[n])
        for n, held in enumerate((up, down, qkv, out_two))
    ]
    loads[0].start()
    loads[1].start()
    back.wait()
    ssm = came_y[...].astype(F32).reshape(features, rows)
    ssm_ref[...] = ssm.astype(BF16)
    gated_ref[...] = (queries_ref[...] * ssm).astype(BF16)
    residual_ref[...] = tokens[...].astype(F32) + contract(
        gated_ref[...], flat_weight(out_all), 0, 0
    )

    gain_rows = all_gains.T
    normed_two[...] = layer_norm(residual_ref[...], gain_rows[1:2]).astype(BF16)
    loads[0].wait()
    for first in range(0, up.shape[2], features):
        own = slice(first, first + features)
        pre = product(normed_two[...], flat_part(up, first, features))
        pre_one[:, own] = pre
        act_one[:, own] = jax.nn.gelu(pre).astype(BF16)
    loads[1].wait()
    down_flat = down[...].reshape(-1, features)
    residual_two[...] = residual_ref[...] + product(act_one[...], down_flat)
    normed_three[...] = layer_norm(residual_two[...], gain_rows[2:3]).astype(BF16)
    gather.run(RUNS[4])
    loads[2].start()
    loads[2].wait()
    y, c, z, x = coordinates()
    me = y * 2 + c
    for first in range(0, 2 * features, features):
        joint = product(normed_three[...], flat_part(qkv, features + first, features))
        att_kv[me, :, first : first + features] = joint.astype(BF16)
    core, side = device_of(y, 1 - c, z, x), device_of(1 - y, c, z, x)

    def pass_on(n, slot, target):
        return pltpu.make_async_remote_copy(
            src_ref=att_kv.at[slot],
            dst_ref=att_kv.at[slot],
            send_sem=line_send.at[n],
            recv_sem=line_recv.at[n],
            device_id=target,
            device_id_type=MESH,
        )

    def taken(n, slot):
        pltpu.make_async_copy(att_kv.at[slot], att_kv.at[slot], line_recv.at[n]).wait()

    far = (1 - y) * 2 + c
    passed = [pass_on(0, me, side), pass_on(1, me, core), pass_on(2, far, core)]
    passed[0].start()
    passed[1].start()
    att_q[...] = product(normed_three[...], flat_part(qkv, 0, features)).astype(BF16)
    taken(0, far)
    passed[2].start()
    gather.run(RUNS[5])
    loads[3].start()
    taken(1, y * 2 + 1 - c)
    taken(2, (1 - y) * 2 + 1 - c)
    keys = blocks * rows
    row_places = me * rows + lax.broadcasted_iota(jnp.int32, (rows, keys), 0)
    key_places = lax.broadcasted_iota(jnp.int32, (rows, keys), 1)
    hidden = jnp.where(key_places <= row_places, key_live[...], 0.0)
    attend_heads(
        hidden > 0.5, att_q, att_kv[...].reshape(keys, 2 * features), attended, log_total
    )
    loads[3].wait()
    residual_three[...] = residual_two[...] + product(attended[...], flat_weight(out_two))
    for each in passed:
        each.wait_send()
    gather.finish()


def first_layer(weights, tokens, live, key_live, mixer, collective_id):
    count = len(weights)
    blocks, groups = lax.axis_size("seq"), lax.axis_size("dp")
    devices = blocks * groups
    rows, features = tokens.shape
    channels = features // devices
    parts = cut([a.shape for a in weights])
    vmem, anywhere = pl.BlockSpec(memory_space=pltpu.VMEM), pl.BlockSpec(memory_space=pl.ANY)
    turned = (features, rows)
    per_channel = (channels, devices, rows)
    results = [
        ((rows, features), F32), (turned, F32), ((8, rows), F32), (turned, BF16), (turned, F32),
        (turned, BF16), (turned, BF16), (per_channel, BF16), (per_channel, BF16), (per_channel, F32),
    ]
    hidden = weights[5].shape[1]
    results += [
        ((rows, features), BF16), ((rows, hidden), F32), ((rows, hidden), BF16),
        ((rows, features), F32), ((rows, features), BF16), ((rows, features), BF16),
        ((blocks, rows, 2 * features), BF16), ((rows, features), BF16), ((rows, 128), F32),
        ((rows, features), F32), ((channels, -(-3 * rows // 128) * 128), F32),
        ((channels, 1, -(-(blocks + 1) * rows // 128) * 128), F32),
    ]
    out = pl.pallas_call(
        partial(first_body, parts, count),
        out_shape=[jax.ShapeDtypeStruct((devices,) + a.shape, a.dtype) for a in weights]
        + [jax.ShapeDtypeStruct(*r) for r in results],
        in_specs=[anywhere] * count + [vmem] * 9,
        out_specs=[vmem] * 5 + [anywhere] * (count - 5) + [vmem] * len(results),
        scratch_shapes=[
            pltpu.VMEM((devices, 2 * channels, rows), F32),
            pltpu.VMEM((devices, 2 * channels, rows), BF16),
            pltpu.VMEM((devices, 2 * channels, rows), BF16),
            pltpu.VMEM((devices, channels, rows), BF16),
            pltpu.VMEM((devices, channels, rows), BF16),
        ]
        + [pltpu.VMEM((devices,) + a.shape, BF16) for a in weights[5:9]]
        + [
            pltpu.VMEM((channels * mixer[1].shape[1], 128), F32),
            pltpu.SemaphoreType.DMA((count,)),
            pltpu.SemaphoreType.DMA((len(parts),)),
            pltpu.SemaphoreType.DMA((len(parts), devices)),
            pltpu.SemaphoreType.DMA((4,)),
            pltpu.SemaphoreType.DMA((4,)),
            pltpu.SemaphoreType.DMA((3,)),
            pltpu.SemaphoreType.DMA((3,)),
        ],
        compiler_params=pltpu.CompilerParams(
            collective_id=collective_id, has_side_effects=True, vmem_limit_bytes=60 * MIB
        ),
    )(*weights, tokens, live, key_live, weights[0], *mixer)
    return out[:count], out[count:]


def mixer_rows(small, mixer, rows, blocks):
    taps, *states = mixer
    kernel, pull = jax.vjp(
        partial(ssm_kernel, length=rows * blocks), *[a.astype(F32) for a in states]
    )
    wide = -(-(blocks + 1) * rows // 128) * 128
    kernel_row = jnp.pad(kernel, ((0, 0), (0, wide - kernel.shape[1])))
    narrow = -(-3 * rows // 128) * 128
    tap_row = jnp.pad(taps.astype(F32), ((0, 0), (0, narrow - taps.shape[1])))
    skip_row = jnp.broadcast_to(small[:, 4:5], small.shape)
    return (tap_row, kernel_row, skip_row), pull


def first_layer_apart(weights, tokens, live, key_live, mixer):
    blocks, groups = lax.axis_size("seq"), lax.axis_size("dp")
    devices = blocks * groups
    rows, features = tokens.shape
    channels = features // devices
    every = [lax.all_gather(a, BOTH, axis=0) for a in weights]
    gain = every[0][:, :, 0].reshape(features, 1)
    key_all, value_all, query_all, out_all = [a.reshape(features, -1) for a in every[1:5]]
    turned = tokens.astype(F32).T
    centered = turned - jnp.mean(turned, axis=0, keepdims=True)
    inverse = lax.rsqrt(jnp.mean(centered * centered, axis=0, keepdims=True) + EPSILON)
    standard = centered * inverse
    normed = (standard * gain).astype(BF16)
    queries = contract(query_all, normed, 0, 0)
    keys = contract(key_all, normed, 0, 0).astype(BF16)
    values = (contract(value_all, normed, 0, 0) * live).astype(BF16)
    sent = jnp.stack([a.reshape(devices, channels, rows) for a in (keys, values)], axis=1)
    k_own, v_own = lax.all_to_all(sent, BOTH, 0, 0, tiled=True).transpose(1, 2, 0, 3)
    per_channel = (channels, devices, rows)
    shifted, mixed = local_call(
        partial(mixer_body, blocks, groups, rows),
        [jax.ShapeDtypeStruct(per_channel, F32), jax.ShapeDtypeStruct(per_channel, BF16)],
        k_own, v_own, *mixer_rows(weights[0], mixer, rows, blocks)[0],
    )
    ssm = lax.all_to_all(mixed.transpose(1, 0, 2), BOTH, 0, 0, tiled=True)
    ssm = ssm.reshape(features, rows)
    gated = (queries * ssm.astype(F32)).astype(BF16)
    residual = tokens.astype(F32) + contract(gated, out_all, 0, 0)
    inverse = jnp.broadcast_to(inverse, (8, rows))
    kept = [residual, standard, inverse, normed, queries, ssm, gated, k_own, v_own, shifted]
    up, down, qkv, out_two = [a.reshape(-1, a.shape[2]) for a in every[5:9]]
    residual_two, stored = feed_forward(residual, every[0][:, :, 1].reshape(features), up, down)
    normed_three = layer_norm(residual_two, every[0][:, :, 2].reshape(features)).astype(BF16)
    joint = product(normed_three, qkv).astype(BF16)
    att_q = joint[:, :features]
    att_kv = lax.all_gather(joint[:, features:], "seq", axis=0)
    where = jnp.stack([lax.axis_index("seq").astype(F32) * rows, jnp.sum(key_live)])
    attended, log_total = local_call(
        attend_body,
        [jax.ShapeDtypeStruct((rows, features), BF16), jax.ShapeDtypeStruct((rows, 128), F32)],
        where.astype(jnp.int32), att_q, att_kv.reshape(blocks * rows, 2 * features), scalars=1,
    )
    residual_three = residual_two + product(attended, out_two)
    kept += [*stored, residual_two, normed_three, att_q, att_kv, attended, log_total]
    return every, kept + [residual_three, None, None]


def mix_back(
    blocks, groups, rows, out_grad, keys, values, shifted, tap_row, kernel_row, skip
):
    span = blocks * rows
    turned = (
        lax.broadcasted_iota(jnp.int32, (rows, rows), 0)
        + lax.broadcasted_iota(jnp.int32, (rows, rows), 1)
        == rows - 1
    ).astype(BF16)

    def lag_sums(earlier, spread, lanes):
        backward = product(earlier, turned).astype(BF16)
        pairs = product_sum(backward, spread)
        padded = jnp.concatenate(
            [pairs, jnp.zeros((rows, lanes - pairs.shape[1]), F32)], axis=1
        )
        return jnp.sum(
            pltpu.roll(padded, lanes - rows + 1, 1, stride=1, stride_axis=0),
            axis=0,
            keepdims=True,
        )

    taps = toeplitz(tap_row, rows)[:, : 2 * rows].astype(BF16)
    longer = toeplitz(kernel_row, rows)[:, :span].astype(BF16)
    values = values.astype(F32)
    signal = shifted * values
    later = block_spread(out_grad, blocks, blocks, groups, rows).astype(BF16)
    signal_grad = product_back(later, longer) + skip * out_grad
    kernel_grad = lag_sums(signal.astype(BF16), later, kernel_row.shape[1])
    skip_grad = jnp.sum(jnp.sum(signal * out_grad, axis=0, keepdims=True), axis=1, keepdims=True)
    shifted_grad = values * signal_grad
    next_two = block_spread(shifted_grad, blocks, 2, groups, rows).astype(BF16)
    return (
        product_back(next_two, taps),
        shifted * signal_grad,
        kernel_grad,
        lag_sums(keys, next_two, tap_row.shape[1]),
        skip_grad,
    )


def mixer_back_body(
    blocks, groups, rows,
    grad_ref, k_ref, v_ref, shifted_ref, taps_ref, kernel_ref, skip_ref,
    grad_k_ref, grad_v_ref, kernel_grad_ref, taps_grad_ref, skip_grad_ref,
):
    for ch in range(k_ref.shape[0]):
        row = slice(ch, ch + 1)
        grad_k, grad_v, kernel_grad_ref[row, :], taps_grad_ref[row, :], skip_grad = mix_back(
            blocks, groups, rows, grad_ref[ch].astype(F32), k_ref[ch], v_ref[ch], shifted_ref[ch],
            taps_ref[row, :], kernel_ref[row, :], skip_ref[row, :1],
        )
        grad_k_ref[ch], grad_v_ref[ch] = grad_k.astype(BF16), grad_v.astype(BF16)
        skip_grad_ref[row, :] = jnp.broadcast_to(skip_grad, (1, 128))


def packed(ref, channels, residual_shape):
    rows, width = residual_shape
    top = 2 * channels

    def at(row, column, height, columns):
        return ref.at[pl.ds(row, height), pl.ds(column, columns)]

    return (
        [
            at(channels, 0, channels, 3 * width),
            at(0, 0, channels, 4 * width),
            at(top, 0, 4 * channels, width),
        ]
        + [at(top + n * channels, width, channels, width) for n in range(4)]
        + [at(top + 5 * channels, width, channels, 128)]
        + [at(top, 2 * width, rows, width)]
        + [at(top + (4 + n) * channels, 0, channels, 64) for n in range(4)]
        + [at(top + 4 * channels, width, channels, 64)]
        + [at(top + 6 * channels, width, channels, 128)]
    )


def last_body(parts, count, kinds, *refs):
    early = refs[:count]
    (
        gain_in, branch, grad_one, live, gated, normed, queries, ssm, standard, inverse,
        gains, key_all, value_all, query_all, out_all,
        k_ref, v_ref, shifted_ref, taps_ref, kernel_ref, small,
    ) = refs[count : count + 21]
    states = refs[count + 21 : count + 25]
    refs = refs[count + 25 :]
    *totals, input_grad, taps_out, s0, s1, s2, s3, skip_grad_ref = packed(
        refs[0], key_all.shape[1], branch.shape
    )
    state_grads = (s0, s1, s2, s3)
    refs = refs[1:]
    out_term, query_term, key_term, value_term, gain_term = own_terms = refs[:5]
    buffers = refs[5 : 5 + 4 * len(parts)]
    refs = refs[5 + 4 * len(parts) :]
    held = dict(zip(kinds, refs[: len(kinds)]))
    (
        wide, sent_g, came_g, sent_kv, came_kv, query_grad, cols, state_sums, kernel_grad_ref,
        taps_grad_ref, send_sem, recv_sem, mine_sem, swap_sem,
    ) = refs[len(kinds) :]
    devices, channels = key_all.shape[0], key_all.shape[1]
    rows, features = branch.shape
    blocks, groups = lax.axis_size("seq"), lax.axis_size("dp")
    greet(all_others()[2])
    reduce = Reduce(
        parts, early + own_terms, totals, buffers, (early, held), send_sem, recv_sem, mine_sem
    )
    reduce.fetch_first()

    def slots(value, columns):
        return value.reshape(2, 2, 4, 2, channels, columns)

    gated_grad = contract(flat_weight(out_all), branch[...], 1, 1)
    sent_g[...] = (gated_grad * queries[...]).reshape(devices, channels, rows).astype(BF16)
    over = Swap(sent_g, came_g, swap_sem.at[0], swap_sem.at[1])
    over.start()
    reduce.start(range(count))
    query_grad[...] = (gated_grad * ssm[...].astype(F32)).astype(BF16)
    out_term[...] = slots(product(gated[...], branch[...]), features).astype(BF16)
    query_term[...] = slots(contract(normed[...], query_grad[...], 1, 1), features).astype(BF16)
    reduce.start((count, count + 1))
    reduce.run(PLACES[0])
    over.wait()
    wide[:, :channels, :] = came_g[...].astype(F32)
    for ch in range(channels):
        row = slice(ch, ch + 1)
        grad_k, grad_v, kernel_grad_ref[ch], taps_grad_ref[row, :], skip_grad = mix_back(
            blocks, groups, rows, wide[:, ch, :], k_ref[ch], v_ref[ch], shifted_ref[ch],
            taps_ref[row, :], kernel_ref[ch], small[row, 4:5],
        )
        wide[:, ch, :], wide[:, channels + ch, :] = grad_k, grad_v
        skip_grad_ref[row, :] = jnp.broadcast_to(skip_grad, (1, 128))
        if ch % 8 == 7:
            reduce.run(PLACES[1 + ch // 8])
    sent_kv[...] = wide[...].astype(BF16)
    back = Swap(sent_kv, came_kv, swap_sem.at[2], swap_sem.at[3])
    back.start()
    taps_out[...] = taps_grad_ref[:, : taps_out.shape[1]]
    grads = kernel_rows_back(
        *[a[...].astype(F32) for a in states], cols, state_sums, kernel_grad_ref, blocks * rows
    )
    for place, grad in zip(state_grads, grads):
        place[...] = grad
    reduce.run(PLACES[4])
    back.wait()
    wide[...] = came_kv[...].astype(F32)
    key_grad = wide[:, :channels, :].reshape(features, rows).astype(BF16)
    value_grad = (wide[:, channels:, :].reshape(features, rows) * live[...]).astype(BF16)
    key_term[...] = slots(contract(normed[...], key_grad, 1, 1), features).astype(BF16)
    value_term[...] = slots(contract(normed[...], value_grad, 1, 1), features).astype(BF16)
    reduce.start((count + 2, count + 3))
    normed_grad = product(flat_weight(query_all), query_grad[...])
    normed_grad += product(flat_weight(key_all), key_grad)
    normed_grad += product(flat_weight(value_all), value_grad)
    gain_grad = jnp.sum(normed_grad * standard[...], axis=1, keepdims=True)
    lane = lax.broadcasted_iota(jnp.int32, (features, 128), 1)
    gain_term[...] = slots(jnp.where(lane == 0, gain_grad, gain_in[...]), 128)
    reduce.start((count + 4,))
    scaled = normed_grad * gains[...].reshape(features, 128)[:, :1]
    scaled = (
        scaled
        - jnp.mean(scaled, axis=0, keepdims=True)
        - standard[...] * jnp.mean(scaled * standard[...], axis=0, keepdims=True)
    )
    input_grad[...] = grad_one[...] + (scaled * inverse[:1, :]).T
    reduce.finish()


def last_layer(
    terms, gain_in, branch, grad_one, live, kept, weights, small, mixer, done, collective_id
):
    standard, inverse, normed, queries, ssm, gated, k_own, v_own, shifted = kept[:9]
    tap_row, kernel_row = kept[9:]
    gains, key_all, value_all, query_all, out_all = weights
    devices, channels, features = key_all.shape
    rows = branch.shape[0]
    count = len(terms)
    square = (channels, features)
    shapes = [a.shape[1:] for a in terms] + [square] * 4 + [(channels, 128)]
    types = [BF16] * (count + 4) + [F32]
    parts = cut(shapes)
    kinds = sorted({(part[2], part[4]) for part in parts if part[0] < count})
    scratch = [pltpu.VMEM((2, 2, 4, 2) + s, t) for s, t in zip(shapes[count:], types[count:])]
    for i, _, part_rows, _, columns, x_last in parts:
        for lead in ((2, 4, 2), (4, 2) if x_last else (2, 4), (4,), (3,)):
            scratch.append(pltpu.VMEM(lead + (part_rows, columns), types[i]))
    scratch += [pltpu.VMEM((2, 2, 4, 2) + kind, BF16) for kind in kinds]
    scratch += [
        pltpu.VMEM((devices, 2 * channels, rows), F32),
        pltpu.VMEM((devices, channels, rows), BF16),
        pltpu.VMEM((devices, channels, rows), BF16),
        pltpu.VMEM((devices, 2 * channels, rows), BF16),
        pltpu.VMEM((devices, 2 * channels, rows), BF16),
        pltpu.VMEM((features, rows), BF16),
        pltpu.VMEM((channels * mixer[1].shape[1], 128), F32),
        pltpu.VMEM((channels * mixer[1].shape[1], 128), F32),
        pltpu.VMEM(kernel_row.shape, F32),
        pltpu.VMEM(tap_row.shape, F32),
        pltpu.SemaphoreType.DMA((len(parts), 6)),
        pltpu.SemaphoreType.DMA((len(parts), 6)),
        pltpu.SemaphoreType.DMA((len(parts),)),
        pltpu.SemaphoreType.DMA((4,)),
    ]
    vmem, anywhere = pl.BlockSpec(memory_space=pltpu.VMEM), pl.BlockSpec(memory_space=pl.ANY)
    height = 2 * channels + max(rows, 8 * channels)
    results = [jax.ShapeDtypeStruct((height, 4 * features), F32)]
    out = pl.pallas_call(
        partial(last_body, parts, count, kinds),
        out_shape=results,
        in_specs=[anywhere] * count + [vmem] * 25,
        out_specs=[vmem] * len(results),
        scratch_shapes=scratch,
        compiler_params=pltpu.CompilerParams(
            collective_id=collective_id, has_side_effects=True, vmem_limit_bytes=62 * MIB
        ),
    )(
        *[a.reshape((2, 2, 4, 2) + a.shape[1:]) for a in terms],
        gain_in, branch, grad_one, live, gated, normed, queries, ssm, standard, inverse,
        gains, key_all, value_all, query_all, out_all,
        k_own, v_own, shifted, tap_row, kernel_row, small, *mixer[1:],
    )
    return settle(done, out[0], channels, (rows, features))


def last_layer_apart(terms, gain_in, branch, grad_one, live, kept, weights, small, mixer):
    standard, inverse, normed, queries, ssm, gated, k_own, v_own, shifted = kept[:9]
    gains, key_all, value_all, query_all, out_all = weights
    devices, channels, features = key_all.shape
    rows = branch.shape[0]
    blocks, groups = lax.axis_size("seq"), lax.axis_size("dp")
    key_all, value_all, query_all, out_all = [
        a.reshape(features, features) for a in (key_all, value_all, query_all, out_all)
    ]
    made, pull = mixer_rows(small, mixer, rows, blocks)
    gated_grad = contract(out_all, branch, 1, 1)
    query_grad = (gated_grad * ssm.astype(F32)).astype(BF16)
    sent = (gated_grad * queries).reshape(devices, channels, rows).astype(BF16)
    own = lax.all_to_all(sent, BOTH, 0, 0, tiled=True).transpose(1, 0, 2)
    per_channel = jax.ShapeDtypeStruct(own.shape, BF16)
    grad_k, grad_v, kernel_grad, taps_grad, skip_grad = local_call(
        partial(mixer_back_body, blocks, groups, rows),
        [per_channel, per_channel]
        + [jax.ShapeDtypeStruct(a.shape, F32) for a in (made[1], made[0])]
        + [jax.ShapeDtypeStruct((channels, 128), F32)],
        own, k_own, v_own, shifted, *made,
    )
    sent = jnp.stack([grad_k.transpose(1, 0, 2), grad_v.transpose(1, 0, 2)], axis=1)
    came = lax.all_to_all(sent, BOTH, 0, 0, tiled=True)
    key_grad = came[:, 0].reshape(features, rows)
    value_grad = (came[:, 1].reshape(features, rows) * live).astype(BF16)
    normed_grad = (
        product(query_all, query_grad) + product(key_all, key_grad) + product(value_all, value_grad)
    )
    gain_grad = jnp.sum(normed_grad * standard, axis=1, keepdims=True)
    lane = lax.broadcasted_iota(jnp.int32, (features, 128), 1)
    gain_term = jnp.where(lane == 0, gain_grad, gain_in)
    scaled = normed_grad * gains.reshape(features, 128)[:, :1]
    scaled = (
        scaled
        - jnp.mean(scaled, axis=0, keepdims=True)
        - standard * jnp.mean(scaled * standard, axis=0, keepdims=True)
    )
    input_grad = grad_one + (scaled * inverse[:1]).T
    last = [product(gated, branch)]
    last += [contract(normed, g, 1, 1) for g in (query_grad, key_grad, value_grad)]
    last = [a.reshape(devices, channels, features).astype(BF16) for a in last]
    last.append(gain_term.reshape(devices, channels, 128))
    sums = [
        lax.psum_scatter(a, BOTH, scatter_dimension=0, tiled=False).astype(F32)
        for a in list(terms) + last
    ]
    taps_grad = taps_grad[:, : mixer[0].shape[1]]
    return sums, [input_grad, taps_grad, *pull(kernel_grad[:, : rows * blocks]), skip_grad]


def allowed_keys(first, length, rows, keys):
    row_places = first + lax.broadcasted_iota(jnp.int32, (rows, keys), 0)
    key_places = lax.broadcasted_iota(jnp.int32, (rows, keys), 1)
    return (key_places <= row_places) & (key_places < length)


def attend_heads(allowed, q_ref, kv, out_ref, log_ref):
    features = q_ref.shape[1]
    for head in range(HEADS):
        own = slice(head * HDIM, (head + 1) * HDIM)
        values = slice(features + head * HDIM, features + (head + 1) * HDIM)
        scores = product_back(q_ref[:, own], kv[:, own]) * HDIM ** (-0.5)
        scores = jnp.where(allowed, scores, MASKED)
        most = jnp.max(scores, axis=1, keepdims=True)
        powers = jnp.exp(scores - most)
        total = jnp.sum(powers, axis=1, keepdims=True)
        weights = (powers * (1.0 / total)).astype(BF16)
        out_ref[:, own] = product(weights, kv[:, values]).astype(BF16)
        log_ref[:, head : head + 1] = most + jnp.log(total)


def attend_body(where_ref, q_ref, kv_ref, out_ref, log_ref):
    allowed = allowed_keys(where_ref[0], where_ref[1], q_ref.shape[0], kv_ref.shape[0])
    attend_heads(allowed, q_ref, kv_ref, out_ref, log_ref)


def attend_back_head(head, allowed, q_ref, kv, log_ref, grad_ref):
    features = q_ref.shape[1]
    scale = HDIM ** (-0.5)
    own = slice(head * HDIM, (head + 1) * HDIM)
    values = slice(features + head * HDIM, features + (head + 1) * HDIM)
    queries, grads = q_ref[:, own], grad_ref[:, own]
    scores = product_back(queries, kv[:, own]) * scale
    probs = jnp.where(allowed, jnp.exp(scores - log_ref[:, head : head + 1]), 0.0)
    prob_grad = product_back(grads, kv[:, values])
    delta = jnp.sum(probs * prob_grad, axis=1, keepdims=True)
    grad_scores = (probs * (prob_grad - delta)).astype(BF16)
    return (
        (product(grad_scores, kv[:, own]) * scale).astype(BF16),
        (product_sum(grad_scores, queries) * scale).astype(BF16),
        product_sum(probs.astype(BF16), grads).astype(BF16),
    )


def attend_back_body(where_ref, q_ref, kv_ref, log_ref, grad_ref, grad_q_ref, grad_kv_ref):
    features = q_ref.shape[1]
    allowed = allowed_keys(where_ref[0], where_ref[1], q_ref.shape[0], kv_ref.shape[0])
    for head in range(HEADS):
        own = slice(head * HDIM, (head + 1) * HDIM)
        values = slice(features + head * HDIM, features + (head + 1) * HDIM)
        grad_q_ref[:, own], grad_kv_ref[:, own], grad_kv_ref[:, values] = attend_back_head(
            head, allowed, q_ref, kv_ref, log_ref, grad_ref
        )


def norm_back(residual, gain_row, grad):
    average = jnp.mean(residual, axis=-1, keepdims=True)
    centered = residual - average
    inverse = lax.rsqrt(jnp.mean(centered * centered, axis=-1, keepdims=True) + EPSILON)
    standard = centered * inverse
    scaled = grad * gain_row
    inner = jnp.mean(scaled * standard, axis=-1, keepdims=True)
    grad_input = inverse * (scaled - jnp.mean(scaled, axis=-1, keepdims=True) - standard * inner)
    return grad_input, jnp.sum(grad * standard, axis=0, keepdims=True)


def middle_body(parts, count, kinds, *refs):
    early = refs[:count]
    qkv_all, up_all, down_all = refs[count : count + 3]
    (
        att_q, att_kv, log_total, grad_attended, key_live, normed_three, residual_two,
        grad_three, gains, act_one, pre_one, normed_two, residual_one,
    ) = refs[count + 3 : count + 16]
    refs = refs[count + 16 :]
    totals = refs[:count]
    qkv_out, up_out, down_out, grad_one, gain_grads = refs[count : count + 5]
    refs = refs[count + 5 :]
    buffers = refs[: 4 * len(parts)]
    refs = refs[4 * len(parts) :]
    held = dict(zip(kinds, refs[: len(kinds)]))
    (
        qkv, up, down, grad_q, grad_kv, line_one, line_two,
        send_sem, recv_sem, mine_sem, load_sem, store_sem, line_send, line_recv,
    ) = refs[len(kinds) :]
    rows, features = att_q.shape
    keys = att_kv.shape[0] * rows
    y, c, z, x = coordinates()
    greet(six_peers(y, c, z, x))
    loads = [
        pltpu.make_async_copy(src, dst, load_sem.at[n])
        for n, (src, dst) in enumerate(((qkv_all, qkv), (up_all, up), (down_all, down)))
    ]
    stores = [
        pltpu.make_async_copy(src, dst, store_sem.at[n])
        for n, (src, dst) in enumerate(((qkv, qkv_out), (up, up_out), (down, down_out)))
    ]
    reduce = Reduce(
        parts, early, totals, buffers, (early, held), send_sem, recv_sem, mine_sem
    )
    reduce.fetch_first()
    reduce.start(range(count))
    for load in loads:
        load.start()
    gain_rows = gains[...].reshape(features, 128).T

    row_places = (y * 2 + c) * rows + lax.broadcasted_iota(jnp.int32, (rows, keys), 0)
    key_places = lax.broadcasted_iota(jnp.int32, (rows, keys), 1)
    allowed = jnp.where(key_places <= row_places, key_live[...], 0.0) > 0.5
    kv = att_kv[...].reshape(keys, 2 * features)
    for head in range(HEADS):
        own = slice(head * HDIM, (head + 1) * HDIM)
        values = slice(features + head * HDIM, features + (head + 1) * HDIM)
        grad_q[:, own], key_grad, value_grad = attend_back_head(
            head, allowed, att_q, kv, log_total, grad_attended
        )
        grad_kv[:, :, :, own] = key_grad.reshape(2, 2, rows, HDIM)
        grad_kv[:, :, :, values] = value_grad.reshape(2, 2, rows, HDIM)
        if head % 4 == 3:
            reduce.run(MIDDLE[head // 4])

    core, side = device_of(y, 1 - c, z, x), device_of(1 - y, c, z, x)

    def line_copy(n, source, target, where):
        return pltpu.make_async_remote_copy(
            src_ref=source,
            dst_ref=where,
            send_sem=line_send.at[n],
            recv_sem=line_recv.at[n],
            device_id=target,
            device_id_type=MESH,
        )

    far = line_copy(0, grad_kv.at[1 - y, 1 - c], core, line_one.at[1 - y])
    near = line_copy(1, grad_kv.at[y, 1 - c], core, line_one.at[y])
    onward = line_copy(2, line_one.at[1 - y], side, line_two)
    far.start()
    near.start()
    far.wait_recv()
    mine = line_one[1 - y].astype(F32) + grad_kv[1 - y, c].astype(F32)
    line_one[1 - y] = mine.astype(BF16)
    onward.start()
    loads[0].wait()
    query_grad = grad_q[...]
    grad_normed = product_back(query_grad, flat_part(qkv, 0, features))
    reduce.run(MIDDLE[3])
    near.wait_recv()
    onward.wait_recv()
    total = (line_one[y].astype(F32) + grad_kv[y, c].astype(F32)) + line_two[...].astype(F32)
    joint = [query_grad, total[:, :features].astype(BF16), total[:, features:].astype(BF16)]
    for n in (1, 2):
        grad_normed += product_back(joint[n], flat_part(qkv, n * features, features))
    grad_from, gain_grad = norm_back(residual_two[...], gain_rows[2:3], grad_normed)
    grad_two = grad_three[...] + grad_from
    gain_grads[...] = jnp.zeros_like(gain_grads)
    gain_grads[2:3, :] = gain_grad
    slots, shard = qkv.shape[0], qkv.shape[1]
    for n in range(3):
        term = product_sum(normed_three[...], joint[n]).reshape(slots, shard, features)
        qkv[:, :, n * features : (n + 1) * features] = term.astype(BF16)
    stores[0].start()
    reduce.run(MIDDLE[4])

    branch = grad_two.astype(BF16)
    loads[1].wait()
    loads[2].wait()
    deep = down.shape[1]
    few = features // deep
    grad_normed = jnp.zeros((rows, features), F32)
    for n in range(up.shape[2] // features):
        own = slice(n * features, (n + 1) * features)
        some = pl.ds(n * few, few)
        gate_grad = product_back(branch, down[some].reshape(features, features))
        pre_grad = jax.vjp(jax.nn.gelu, pre_one[:, own])[1](gate_grad)[0].astype(BF16)
        grad_normed += product_back(pre_grad, flat_part(up, n * features, features))
        term = product_sum(act_one[:, own], branch)
        down[some] = term.astype(BF16).reshape(few, deep, features)
        term = product_sum(normed_two[...], pre_grad).reshape(slots, shard, features)
        up[:, :, own] = term.astype(BF16)
        reduce.run(MIDDLE[5 + n])
    stores[1].start()
    stores[2].start()
    grad_from, gain_grad = norm_back(residual_one[...], gain_rows[1:2], grad_normed)
    grad_one[...] = grad_two + grad_from
    gain_grads[1:2, :] = gain_grad
    reduce.finish()
    for each in (far, near, onward):
        each.wait_send()
    for store in stores:
        store.wait()


def middle_layers(terms, weights, kept, collective_id):
    count = len(terms)
    att_q, act_one = kept[0], kept[9]
    rows, features = att_q.shape
    shapes = [a.shape[1:] for a in terms]
    parts = cut(shapes)
    kinds = sorted({(part[2], part[4]) for part in parts})
    scratch = []
    for _, _, part_rows, _, columns, x_last in parts:
        for lead in ((2, 4, 2), (4, 2) if x_last else (2, 4), (4,), (3,)):
            scratch.append(pltpu.VMEM(lead + (part_rows, columns), BF16))
    scratch += [pltpu.VMEM((2, 2, 4, 2) + kind, BF16) for kind in kinds]
    scratch += [pltpu.VMEM(a.shape, BF16) for a in weights]
    scratch += [
        pltpu.VMEM((rows, features), BF16),
        pltpu.VMEM((2, 2, rows, 2 * features), BF16),
        pltpu.VMEM((2, rows, 2 * features), BF16),
        pltpu.VMEM((rows, 2 * features), BF16),
        pltpu.SemaphoreType.DMA((len(parts), 6)),
        pltpu.SemaphoreType.DMA((len(parts), 6)),
        pltpu.SemaphoreType.DMA((len(parts),)),
        pltpu.SemaphoreType.DMA((3,)),
        pltpu.SemaphoreType.DMA((3,)),
        pltpu.SemaphoreType.DMA((3,)),
        pltpu.SemaphoreType.DMA((3,)),
    ]
    vmem, anywhere = pl.BlockSpec(memory_space=pltpu.VMEM), pl.BlockSpec(memory_space=pl.ANY)
    results = [jax.ShapeDtypeStruct(s, F32) for s in shapes]
    results += [jax.ShapeDtypeStruct(a.shape, BF16) for a in weights]
    results += [
        jax.ShapeDtypeStruct((rows, features), F32),
        jax.ShapeDtypeStruct((8, features), F32),
    ]
    out = pl.pallas_call(
        partial(middle_body, parts, count, kinds),
        out_shape=results,
        in_specs=[anywhere] * (count + 3) + [vmem] * 13,
        out_specs=[vmem] * count + [anywhere] * 3 + [vmem] * 2,
        scratch_shapes=scratch,
        compiler_params=pltpu.CompilerParams(
            collective_id=collective_id, has_side_effects=True, vmem_limit_bytes=60 * MIB
        ),
    )(*[a.reshape((2, 2, 4, 2) + a.shape[1:]) for a in terms], *weights, *kept)
    return out[:count], out[count : count + 3], out[count + 3], out[count + 4]


def local_call(body, out_shape, *operands, scalars=0, limit=48):
    vmem = pl.BlockSpec(memory_space=pltpu.VMEM)
    smem = pl.BlockSpec(memory_space=pltpu.SMEM)
    return pl.pallas_call(
        body,
        out_shape=out_shape,
        in_specs=[smem] * scalars + [vmem] * (len(operands) - scalars),
        out_specs=jax.tree.map(lambda _: vmem, out_shape),
        compiler_params=pltpu.CompilerParams(vmem_limit_bytes=limit * MIB),
    )(*operands)


def settle(done, everything, channels, residual_shape):
    width = residual_shape[1]
    shapes = [a.shape for a in done]
    shapes += [(channels, 3 * width), (channels, 4 * width), (4 * channels, width)]
    shapes += [(channels, width)] * 4 + [(channels, 128), residual_shape]
    shapes += [(channels, 64)] * 5 + [(channels, 128)]
    count = len(done)

    def body(*refs):
        sources = [*refs[:count], *packed(refs[count], channels, residual_shape)]
        for source, place in zip(sources, refs[count + 1 :]):
            place[...] = source[...]

    out = local_call(
        body, [jax.ShapeDtypeStruct(s, F32) for s in shapes], *done, everything
    )
    return out[: count + 8], out[count + 8 :]


def shards(
    tokens, lengths, norm_one, query_one, key_one, value_one, shift_taps, decay_log,
    turn_angle, mix_real, mix_imag, skip_gain, out_one, norm_two, up_one, down_one,
    norm_three, qkv_weight, out_two, norm_four, up_two, down_two, cotangent,
):
    blocks, groups = lax.axis_size("seq"), lax.axis_size("dp")
    devices = blocks * groups
    rows, features = tokens.shape[1], tokens.shape[2]
    channels = features // devices
    place = lax.axis_index("seq")
    length = lengths[0]
    row_places = place * rows + jnp.arange(rows, dtype=jnp.int32)
    live_mask = (row_places < length).astype(F32)[:, None]
    live_lane = (row_places < length).astype(F32)[None, :]

    small = jnp.stack([norm_one, norm_two, norm_three, norm_four, skip_gain], axis=1)
    small = jnp.pad(small.astype(F32), ((0, 0), (0, 123)))
    mixer = [shift_taps, decay_log, turn_angle, mix_real, mix_imag]
    weights = [
        small, key_one, value_one, query_one, out_one, up_one, down_one, qkv_weight, out_two,
        up_two, down_two,
    ]
    key_live = (jnp.arange(blocks * rows, dtype=jnp.int32) < length).astype(F32)[None, :]
    if grouped():
        every, kept = first_layer(weights, tokens[0], live_lane, key_live, mixer, 1)
    else:
        every, kept = first_layer_apart(weights, tokens[0], live_lane, key_live, mixer)
    residual_one = kept[0]
    gain_one, gain_two, gain_three, gain_four = [
        every[0][:, :, n].reshape(features) for n in range(4)
    ]
    up_one_all, down_one_all, qkv_all, out_two_all, late_up, late_down = [
        g.reshape((-1, g.shape[2])) for g in every[5:]
    ]

    normed_two, pre_one, act_one, residual_two, normed_three, att_q, kv = kept[10:17]
    attended, log_total, residual_three = kept[17:20]
    residual_four, stored_four = feed_forward(residual_three, gain_four, late_up, late_down)
    activations = (live_mask * residual_four).astype(BF16)

    grad_four = live_mask * cotangent[0].astype(F32)
    grad_three, grad_norm_four, grad_up_two, grad_down_two = feed_back(
        residual_three, gain_four, late_up, late_down, stored_four, grad_four
    )
    branch_three = grad_three.astype(BF16)
    grad_out_two = product_sum(attended, branch_three)
    grad_attended = product_back(branch_three, out_two_all).astype(BF16)
    slots = (devices, -1)
    terms = [
        g.astype(BF16).reshape(slots + g.shape[1:])
        for g in (grad_up_two, grad_down_two, grad_out_two)
    ]
    if grouped():
        done, terms, grad_one, gain_grads = middle_layers(
            terms,
            every[7:8] + every[5:7],
            [
                att_q, kv, log_total, grad_attended, key_live, normed_three, residual_two,
                grad_three, every[0], act_one, pre_one, normed_two, residual_one,
            ],
            3,
        )
        grad_norm_two, grad_norm_three = gain_grads[1], gain_grads[2]
    else:
        grad_q, grad_kv = local_call(
            attend_back_body,
            [
                jax.ShapeDtypeStruct((rows, features), BF16),
                jax.ShapeDtypeStruct((blocks * rows, 2 * features), BF16),
            ],
            jnp.stack([place.astype(jnp.int32) * rows, length]), att_q,
            kv.reshape(blocks * rows, 2 * features), log_total, grad_attended, scalars=1,
        )
        grad_kv = lax.psum_scatter(
            grad_kv.reshape(blocks, rows, 2 * features), "seq", scatter_dimension=0
        )
        grad_joint = jnp.concatenate([grad_q, grad_kv.astype(BF16)], axis=1)
        grad_qkv_weight = product_sum(normed_three, grad_joint)
        grad_normed_three = product_back(grad_joint, qkv_all)
        grad_from_three, grad_norm_three = jax.vjp(layer_norm, residual_two, gain_three)[1](
            grad_normed_three
        )
        grad_one, grad_norm_two, grad_up_one, grad_down_one = feed_back(
            residual_one, gain_two, up_one_all, down_one_all, (normed_two, pre_one, act_one),
            grad_three + grad_from_three,
        )
        done = []
        terms += [
            g.astype(BF16).reshape(slots + g.shape[1:])
            for g in (grad_qkv_weight, grad_up_one, grad_down_one)
        ]
    branch_one = grad_one.astype(BF16)
    gain_in = jnp.stack(
        [jnp.zeros_like(grad_norm_two), grad_norm_two, grad_norm_three, grad_norm_four], axis=1
    )
    gain_in = jnp.pad(gain_in, ((0, 0), (0, 124)))
    last = (
        terms, gain_in, branch_one, grad_one, live_lane, kept[1:10] + kept[20:], every[:5], small,
        mixer,
    )
    if grouped():
        sums, rest = last_layer(*last, done, 2)
    else:
        sums, rest = last_layer_apart(*last)
    grad_up_two, grad_down_two, grad_out_two, grad_qkv_weight, grad_up_one, grad_down_one = sums[:6]
    grad_out_one, grad_query_one, grad_key_one, grad_value_one, gain_grads = sums[6:]
    gain_grads = gain_grads[:, :4].T
    input_grad, grad_shift_taps, grad_decay_log, grad_turn_angle, grad_mix_real = rest[:5]
    grad_mix_imag, skip_grad = rest[5:]
    grad_skip_gain = skip_grad[:, 0]
    return (
        activations[None], input_grad[None],
        gain_grads[0], grad_query_one, grad_key_one, grad_value_one,
        grad_shift_taps, grad_decay_log, grad_turn_angle, grad_mix_real, grad_mix_imag,
        grad_skip_gain, grad_out_one,
        gain_grads[1], grad_up_one, grad_down_one,
        gain_grads[2], grad_qkv_weight, grad_out_two,
        gain_grads[3], grad_up_two, grad_down_two,
    )


def solution(mesh):
    row, vector = P(BOTH, None), P(BOTH)
    whole = P("dp", "seq", None)
    weights = (
        vector, row, row, row, row, row, row, row, row, vector, row,
        vector, row, row, vector, row, row, vector, row, row,
    )
    return jax.shard_map(
        shards,
        mesh=mesh,
        in_specs=(whole, P("dp")) + weights + (whole,),
        out_specs=(whole, whole) + weights,
        check_vma=False,
    )
```

profile of v0, /device:TPU:0, one launch (start us, length us, event | category | flops | bytes accessed | tf_op | source)
XLA Modules:
  0.0 415.2 jit_solution(425185607958630378)
XLA Ops:
  1.3 0.6 compare_convert_fusion.1.refs_12_.refs_6_
  1.9 0.7 stack.29
  2.6 0.6 compare_convert_fusion.refs_13_.refs_10_
  3.2 0.1 copy.58
  3.3 0.6 pad_convert_fusion.refs_0_.refs_14_.refs_23_
  3.9 178.5 %shard_map.390 = (f32[32,24,128]{2,1,0:T(8,128)}, bf16[32,24,768]{2,1,0:T(8,128)(2,1)}, bf16[32,24,768]{2,1,0:T(8,128)(2,1)}, bf16[32,24,768]{2,1,0:T(8,128)(2,1...) custom-call(f32[24,128]{1,0:T(8,128)} %pad_convert_fusion.refs_0_.re, ...), custom_call_target="tpu_custom_call" | custom-call | tf_op jit(solution)/shard_map/pallas_call | solution.py:731
  182.4 1.2 reduce_sum.43
  183.7 1.3 multiply_reduce_fusion.2
  185.0 1.3 slice_reduce_fusion
  186.3 0.1 mul.137
  186.4 3.5 fusion.25
  189.9 5.1 %fusion.9 = bf16[1,192,768]{2,1,0:T(8,128)(2,1)} fusion(f32[192,768]{1,0:T(8,128)S(1)} %copy-done.4, bf16[3072,768]{1,0:T(8,128)(2,1)} %bitcast.68, f32[192]{0:T(256)S(1)} %compare_convert_fusion.2, f32[192,3072]{1,0:T(8,128)S(1)} %fusion.25), kind=kOutput, calls=%fused_computation.17 | convolution fusion | flops 911720448 | bytes 7963392 | tf_op jit(solution)/shard_map/dot_general | solution.py:364
  195.0 4.8 %fusion.6 = bf16[192,3072]{1,0:T(8,128)(2,1)S(1)} fusion(f32[192,3072]{1,0:T(8,128)S(1)} %fusion.25, bf16[3072,768]{1,0:T(8,128)(2,1)} %bitcast.69, bf16[1,192,768]{2,1,0:T(8,128)(2,1)S(1)} %copy-done.7, f32[192]{0:T(256)S(1)} %compare_convert_fusion.2), kind=kOutput, calls=%fused_computation.10 | convolution fusion | flops 918208512 | bytes 8553216 | tf_op jit(solution)/shard_map/dot_general | solution.py:364
  199.9 1.9 multiply_reduce_fusion
  201.8 0.3 fusion.26
  202.1 0.2 fusion.12.refs_13_
  202.3 0.8 copy-done.6
  203.0 1.3 convolution_convert_fusion.3.refs_9_
  204.3 1.6 convolution_convert_fusion.2
  205.9 4.3 %convolution_convert_fusion = bf16[3072,768]{1,0:T(8,128)(2,1)} fusion(bf16[1,192,768]{2,1,0:T(8,128)(2,1)S(1)} %copy-done.7, f32[192]{0:T(256)S(1)} %compare_convert_fusion.2, f32[192,3072]{1,0:T(8,128)S(1)} %fusion.25), kind=kOutput, calls=%fused_computation | convolution fusion | flops 914079744 | bytes 7373568 | tf_op jit(solution)/shard_map/dot_general | solution.py:364
  210.2 3.7 convolution_convert_fusion.1
  213.9 83.0 %shard_map.391 = (f32[24,3072]{1,0:T(8,128)}, f32[96,768]{1,0:T(8,128)}, f32[24,768]{1,0:T(8,128)}, bf16[32,24,2304]{2,1,0:T(8,128)(2,1)}, bf16[32,24,3072]{2,1,...) custom-call(bf16[2,2,4,2,24,3072]{5,4,3,2,1,0:T(8,128)(2,1)} %bitcast.51, ...), custom_call_target="tpu_custom_call" | custom-call | tf_op jit(solution)/shard_map/pallas_call | solution.py:1321
  296.9 0.8 slice_bitcast_fusion.2
  297.7 0.1 pad_maximum_fusion
  297.8 1.8 convert_element_type.97.refs_4_
  299.6 0.2 copy.59
  299.8 0.8 pad.12.refs_3_
  300.6 109.6 %shard_map.392.refs_3_ = f32[240,3072]{1,0:T(8,128)} custom-call(bf16[2,2,4,2,24,2304]{5,4,3,2,1,0:T(8,128)(2,1)} %bitcast.60, bf16[2,2,4,2,24,3072]{5,4,3,2,1,0:T(8,128)(2,1)} %bitcast.57, bf16[2,2,4,2,96,768]{5,4,3,2,1,0:T(8,128)(2,1)} %bitcast.58, f32[768,128]{1,0:T(8,128)} %pad.12.refs_3_, bf16[192,768]{1,0:T(8,128)(2,1)} %convert_element_type.97.refs_4_, ...), custom_call_target="tpu_custom_call" | custom-call | tf_op jit(solution)/shard_map/pallas_call | solution.py:1028
  410.2 1.8 copy-done
  412.1 1.6 shard_map.393
  413.6 0.6 slice_reduce_fusion.5
  414.3 0.7 slice_reduce_fusion.1
  (29 shorter events, 0.1 us)
Async XLA Ops:
  182.4 4.0 copy-start.4
  189.9 5.2 %copy-start.7 = (bf16[1,192,768]{2,1,0:T(8,128)(2,1)S(1)}, bf16[1,192,768]{2,1,0:T(8,128)(2,1)}, u32[]{:S(2)}) copy-start(bf16[1,192,768]{2,1,0:T(8,128)(2,1)} %param.45) | copy-start | bytes 884740
  189.9 10.0 %slice-start = ((s8[4718592]{0:T(1024)(128)(4,1)}), s8[4194304]{0:T(1024)(128)(4,1)S(1)}, s32[]{:S(2)}) async-start(s8[4718592]{0:T(1024)(128)(4,1)} %bitcast.53), calls=%async_computation | async-start | bytes 8388608
  195.0 4.8 %slice-start.1 = ((s8[4718592]{0:T(1024)(128)(4,1)}), s8[524288]{0:T(1024)(128)(4,1)S(1)}, s32[]{:S(2)}) async-start(s8[4718592]{0:T(1024)(128)(4,1)} %bitcast.53), calls=%async_computation.1 | async-start | bytes 1048576
  201.8 1.3 copy-start.6
  201.8 2.5 copy-start.8
  203.0 7.1 %copy-start.5 = (f32[192,768]{1,0:T(8,128)}, f32[192,768]{1,0:T(8,128)S(1)}, u32[]{:S(2)}) copy-start(f32[192,768]{1,0:T(8,128)S(1)} %fusion.12.refs_13_) | copy-start | bytes 1769476
  300.5 109.7 %copy-start.1 = (f32[24,3072]{1,0:T(8,128)S(1)}, f32[24,3072]{1,0:T(8,128)}, u32[]{:S(2)}) copy-start(f32[24,3072]{1,0:T(8,128)} %get-tuple-element.99.refs_0_) | copy-start | bytes 884740
  300.5 109.7 %copy-start.2 = (f32[96,768]{1,0:T(8,128)S(1)}, f32[96,768]{1,0:T(8,128)}, u32[]{:S(2)}) copy-start(f32[96,768]{1,0:T(8,128)} %get-tuple-element.100.refs_1_) | copy-start | bytes 884740
  300.6 109.7 %copy-start.3 = (f32[24,768]{1,0:T(8,128)S(1)}, f32[24,768]{1,0:T(8,128)}, u32[]{:S(2)}) copy-start(f32[24,768]{1,0:T(8,128)} %get-tuple-element.101.refs_2_) | copy-start | bytes 221188
  410.2 1.8 copy-start
where the time goes:
time: 418 us; the launch traced here: 415 us
  Pallas kernels  373 us (89%)
  matrix products  26.1 us (6%)
  local copies, waits for them, and re-layouts  8.01 us (2%)
  other arithmetic  6.65 us (2%)
    pallas_call x1, Pallas kernels, first_layer(): pl.pallas_call(partial(first_body, parts, count), out_shape=[jax.ShapeDty...  178 us
    pallas_call x1, Pallas kernels, last_layer(): pl.pallas_call(partial(last_body, parts, count, kinds), out_shape=results...  110 us
    pallas_call x1, Pallas kernels, middle_layers(): pl.pallas_call(partial(middle_body, parts, count, kinds), out_shape=resul...  83 us
    dot_general x8, matrix products, contract(): lax.dot_general(left_side, right_side, (((left_dim,), (right_dim,)), ((),...  26.1 us

commit v1 on v0

--- a/solution.py
+++ b/solution.py
@@ -19,8 +19,8 @@
 PLACES = (4, 5, 6, 7, 9)
 MIDDLE = (1, 1, 2, 3, 4, 5, 6, 7, 8)
 EARLY = 2
-RUNS = (8, 11, 12, 14, 15, 17)
-AHEAD = 4
+RUNS = (8, 9, 9, 10, 11, 12)
+AHEAD = 5
 F32 = jnp.float32
 BF16 = jnp.bfloat16
 
@@ -575,12 +575,12 @@
         residual_ref, standard_ref, inverse_ref, normed_ref, queries_ref, ssm_ref, gated_ref,
         k_ref, v_ref, shifted_ref,
         normed_two, pre_one, act_one, residual_two, normed_three, att_q, att_kv, attended,
-        log_total, residual_three, taps_ref, kernel_ref,
-    ) = refs[count : count + 22]
+        log_total, residual_three, taps_ref, kernel_ref, gain_out,
+    ) = refs[count : count + 23]
     (
         wide, sent_kv, came_kv, sent_y, came_y, up, down, qkv, out_two, cols,
         local_sem, send_sem, recv_sem, swap_sem, load_sem, line_send, line_recv,
-    ) = refs[count + 22 :]
+    ) = refs[count + 23 :]
     gains, key_all, value_all, query_all, out_all = gathered[:5]
     devices, channels = key_all.shape[0], key_all.shape[1]
     rows, features = tokens.shape
@@ -647,6 +647,7 @@
     )
 
     gain_rows = all_gains.T
+    gain_out[...] = gain_rows[:8]
     normed_two[...] = layer_norm(residual_ref[...], gain_rows[1:2]).astype(BF16)
     loads[0].wait()
     for first in range(0, up.shape[2], features):
@@ -712,7 +713,9 @@
     devices = blocks * groups
     rows, features = tokens.shape
     channels = features // devices
-    parts = cut([a.shape for a in weights])
+    parts = [
+        (n, 0, a.shape[0], 0, a.shape[1], n % 2 == 0) for n, a in enumerate(weights)
+    ]
     vmem, anywhere = pl.BlockSpec(memory_space=pltpu.VMEM), pl.BlockSpec(memory_space=pl.ANY)
     turned = (features, rows)
     per_channel = (channels, devices, rows)
@@ -726,7 +729,7 @@
         ((rows, features), F32), ((rows, features), BF16), ((rows, features), BF16),
         ((blocks, rows, 2 * features), BF16), ((rows, features), BF16), ((rows, 128), F32),
         ((rows, features), F32), ((channels, -(-3 * rows // 128) * 128), F32),
-        ((channels, 1, -(-(blocks + 1) * rows // 128) * 128), F32),
+        ((channels, 1, -(-(blocks + 1) * rows // 128) * 128), F32), ((8, features), F32),
     ]
     out = pl.pallas_call(
         partial(first_body, parts, count),
@@ -816,7 +819,8 @@
     )
     residual_three = residual_two + product(attended, out_two)
     kept += [*stored, residual_two, normed_three, att_q, att_kv, attended, log_total]
-    return every, kept + [residual_three, None, None]
+    gain_rows = every[0][:, :, :8].reshape(features, 8).T
+    return every, kept + [residual_three, None, None, gain_rows]
 
 
 def mix_back(
@@ -975,7 +979,8 @@
     normed_grad += product(flat_weight(value_all), value_grad)
     gain_grad = jnp.sum(normed_grad * standard[...], axis=1, keepdims=True)
     lane = lax.broadcasted_iota(jnp.int32, (features, 128), 1)
-    gain_term[...] = slots(jnp.where(lane == 0, gain_grad, gain_in[...]), 128)
+    others = jnp.concatenate([gain_in[...].T, jnp.zeros((features, 120), F32)], axis=1)
+    gain_term[...] = slots(jnp.where(lane == 0, gain_grad, others), 128)
     reduce.start((count + 4,))
     scaled = normed_grad * gains[...].reshape(features, 128)[:, :1]
     scaled = (
@@ -1074,7 +1079,7 @@
     )
     gain_grad = jnp.sum(normed_grad * standard, axis=1, keepdims=True)
     lane = lax.broadcasted_iota(jnp.int32, (features, 128), 1)
-    gain_term = jnp.where(lane == 0, gain_grad, gain_in)
+    gain_term = jnp.where(lane == 0, gain_grad, jnp.pad(gain_in.T, ((0, 0), (0, 120))))
     scaled = normed_grad * gains.reshape(features, 128)[:, :1]
     scaled = (
         scaled
@@ -1165,12 +1170,12 @@
     qkv_all, up_all, down_all = refs[count : count + 3]
     (
         att_q, att_kv, log_total, grad_attended, key_live, normed_three, residual_two,
-        grad_three, gains, act_one, pre_one, normed_two, residual_one,
-    ) = refs[count + 3 : count + 16]
-    refs = refs[count + 16 :]
+        grad_three, gain_rows, act_one, pre_one, normed_two, residual_one, fourth,
+    ) = refs[count + 3 : count + 17]
+    refs = refs[count + 17 :]
     totals = refs[:count]
-    qkv_out, up_out, down_out, grad_one, gain_grads = refs[count : count + 5]
-    refs = refs[count + 5 :]
+    qkv_out, up_out, down_out, grad_one, gain_grads, branch_out = refs[count : count + 6]
+    refs = refs[count + 6 :]
     buffers = refs[: 4 * len(parts)]
     refs = refs[4 * len(parts) :]
     held = dict(zip(kinds, refs[: len(kinds)]))
@@ -1197,8 +1202,6 @@
     reduce.start(range(count))
     for load in loads:
         load.start()
-    gain_rows = gains[...].reshape(features, 128).T
-
     row_places = (y * 2 + c) * rows + lax.broadcasted_iota(jnp.int32, (rows, keys), 0)
     key_places = lax.broadcasted_iota(jnp.int32, (rows, keys), 1)
     allowed = jnp.where(key_places <= row_places, key_live[...], 0.0) > 0.5
@@ -1248,6 +1251,7 @@
     grad_from, gain_grad = norm_back(residual_two[...], gain_rows[2:3], grad_normed)
     grad_two = grad_three[...] + grad_from
     gain_grads[...] = jnp.zeros_like(gain_grads)
+    gain_grads[3:4, :] = fourth[...]
     gain_grads[2:3, :] = gain_grad
     slots, shard = qkv.shape[0], qkv.shape[1]
     for n in range(3):
@@ -1277,6 +1281,7 @@
     stores[2].start()
     grad_from, gain_grad = norm_back(residual_one[...], gain_rows[1:2], grad_normed)
     grad_one[...] = grad_two + grad_from
+    branch_out[...] = grad_one[...].astype(BF16)
     gain_grads[1:2, :] = gain_grad
     reduce.finish()
     for each in (far, near, onward):
@@ -1317,18 +1322,19 @@
     results += [
         jax.ShapeDtypeStruct((rows, features), F32),
         jax.ShapeDtypeStruct((8, features), F32),
+        jax.ShapeDtypeStruct((rows, features), BF16),
     ]
     out = pl.pallas_call(
         partial(middle_body, parts, count, kinds),
         out_shape=results,
-        in_specs=[anywhere] * (count + 3) + [vmem] * 13,
-        out_specs=[vmem] * count + [anywhere] * 3 + [vmem] * 2,
+        in_specs=[anywhere] * (count + 3) + [vmem] * 14,
+        out_specs=[vmem] * count + [anywhere] * 3 + [vmem] * 3,
         scratch_shapes=scratch,
         compiler_params=pltpu.CompilerParams(
             collective_id=collective_id, has_side_effects=True, vmem_limit_bytes=60 * MIB
         ),
     )(*[a.reshape((2, 2, 4, 2) + a.shape[1:]) for a in terms], *weights, *kept)
-    return out[:count], out[count : count + 3], out[count + 3], out[count + 4]
+    return out[:count], out[count : count + 3], *out[count + 3 :]
 
 
 def local_call(body, out_shape, *operands, scalars=0, limit=48):
@@ -1390,9 +1396,8 @@
     else:
         every, kept = first_layer_apart(weights, tokens[0], live_lane, key_live, mixer)
     residual_one = kept[0]
-    gain_one, gain_two, gain_three, gain_four = [
-        every[0][:, :, n].reshape(features) for n in range(4)
-    ]
+    gain_rows = kept[22]
+    gain_two, gain_three, gain_four = gain_rows[1], gain_rows[2], gain_rows[3]
     up_one_all, down_one_all, qkv_all, out_two_all, late_up, late_down = [
         g.reshape((-1, g.shape[2])) for g in every[5:]
     ]
@@ -1415,16 +1420,16 @@
         for g in (grad_up_two, grad_down_two, grad_out_two)
     ]
     if grouped():
-        done, terms, grad_one, gain_grads = middle_layers(
+        done, terms, grad_one, gain_in, branch_one = middle_layers(
             terms,
             every[7:8] + every[5:7],
             [
                 att_q, kv, log_total, grad_attended, key_live, normed_three, residual_two,
-                grad_three, every[0], act_one, pre_one, normed_two, residual_one,
+                grad_three, gain_rows, act_one, pre_one, normed_two, residual_one,
+                grad_norm_four[None],
             ],
             3,
         )
-        grad_norm_two, grad_norm_three = gain_grads[1], gain_grads[2]
     else:
         grad_q, grad_kv = local_call(
             attend_back_body,
@@ -1453,13 +1458,13 @@
             g.astype(BF16).reshape(slots + g.shape[1:])
             for g in (grad_qkv_weight, grad_up_one, grad_down_one)
         ]
-    branch_one = grad_one.astype(BF16)
-    gain_in = jnp.stack(
-        [jnp.zeros_like(grad_norm_two), grad_norm_two, grad_norm_three, grad_norm_four], axis=1
-    )
-    gain_in = jnp.pad(gain_in, ((0, 0), (0, 124)))
+        branch_one = grad_one.astype(BF16)
+        gain_in = jnp.stack(
+            [jnp.zeros_like(grad_norm_two), grad_norm_two, grad_norm_three, grad_norm_four]
+        )
+        gain_in = jnp.pad(gain_in, ((0, 4), (0, 0)))
     last = (
-        terms, gain_in, branch_one, grad_one, live_lane, kept[1:10] + kept[20:], every[:5], small,
+        terms, gain_in, branch_one, grad_one, live_lane, kept[1:10] + kept[20:22], every[:5], small,
         mixer,
     )
     if grouped():

time: 418 us -> 405 us (0.969)
  Pallas kernels: 373 us -> 368 us
  matrix products: 26.1 us -> 21.5 us
    dot_general x8, matrix products: 26.1 us -> 21.5 us  [contract(): lax.dot_general(left_side, right_side, (((left_dim,), (right_dim,)), ((),...]
where the time goes in v1:
time: 405 us; the launch traced here: 402 us
  Pallas kernels  368 us (91%)
  matrix products  21.5 us (5%)
  local copies, waits for them, and re-layouts  5.62 us (1%)
  other arithmetic  4.86 us (1%)
    pallas_call x1, Pallas kernels, first_layer(): pl.pallas_call(partial(first_body, parts, count), out_shape=[jax.ShapeDty...  176 us
    pallas_call x1, Pallas kernels, last_layer(): pl.pallas_call(partial(last_body, parts, count, kinds), out_shape=results...  109 us
    pallas_call x1, Pallas kernels, middle_layers(): pl.pallas_call(partial(middle_body, parts, count, kinds), out_shape=resul...  81.5 us
    dot_general x8, matrix products, contract(): lax.dot_general(left_side, right_side, (((left_dim,), (right_dim,)), ((),...  21.5 us

profile of v1, /device:TPU:0, one launch (start us, length us, event | category | flops | bytes accessed | tf_op | source)
XLA Modules:
  0.0 401.9 jit_solution(3729710638030085958)
XLA Ops:
  1.3 0.6 compare_convert_fusion.1.refs_12_.refs_6_
  1.9 0.7 stack.23
  2.6 0.6 compare_convert_fusion.refs_13_.refs_10_
  3.2 0.1 copy.55
  3.3 0.6 pad_convert_fusion.refs_0_.refs_14_.refs_23_
  3.9 175.6 %shard_map.390 = (f32[32,24,128]{2,1,0:T(8,128)}, bf16[32,24,768]{2,1,0:T(8,128)(2,1)}, bf16[32,24,768]{2,1,0:T(8,128)(2,1)}, bf16[32,24,768]{2,1,0:T(8,128)(2,1...) custom-call(f32[24,128]{1,0:T(8,128)} %pad_convert_fusion.refs_0_.re, ...), custom_call_target="tpu_custom_call" | custom-call | tf_op jit(solution)/shard_map/pallas_call | solution.py:734
  179.5 1.2 reduce_sum.43
  180.7 0.0 slice-start.2
  180.7 1.4 multiply_reduce_fusion.2
  182.2 0.8 slice_reduce_fusion.5
  182.9 0.0 slice-start.3
  182.9 3.7 fusion.25
  186.7 0.0 copy-start.7
  186.8 0.0 slice-start
  186.8 2.2 fusion.9
  189.0 0.0 copy-done.7
  189.0 2.9 fusion.6
  191.9 1.9 multiply_reduce_fusion
  193.8 0.6 reshape.133.refs_19_
  194.4 0.3 fusion.26
  194.7 0.2 fusion.12.refs_13_
  194.8 0.2 copy-done.6
  195.0 1.3 convolution_convert_fusion.3.refs_9_
  196.3 1.6 convolution_convert_fusion.2
  197.9 4.3 %convolution_convert_fusion = bf16[3072,768]{1,0:T(8,128)(2,1)} fusion(bf16[1,192,768]{2,1,0:T(8,128)(2,1)S(1)} %copy-done.7, f32[192]{0:T(256)S(1)} %compare_convert_fusion.2, f32[192,3072]{1,0:T(8,128)S(1)} %fusion.25), kind=kOutput, calls=%fused_computation | convolution fusion | flops 914079744 | bytes 7373568 | tf_op jit(solution)/shard_map/dot_general | solution.py:364
  202.2 3.7 convolution_convert_fusion.1
  205.9 81.5 %shard_map.391 = (f32[24,3072]{1,0:T(8,128)}, f32[96,768]{1,0:T(8,128)}, f32[24,768]{1,0:T(8,128)}, bf16[32,24,2304]{2,1,0:T(8,128)(2,1)}, bf16[32,24,3072]{2,1,...) custom-call(bf16[2,2,4,2,24,3072]{5,4,3,2,1,0:T(8,128)(2,1)} %bitcas, ...), custom_call_target="tpu_custom_call" | custom-call | tf_op jit(solution)/shard_map/pallas_call | solution.py:1327
  287.5 109.4 %shard_map.392.refs_3_ = f32[240,3072]{1,0:T(8,128)} custom-call(bf16[2,2,4,2,24,2304]{5,4,3,2,1,0:T(8,128)(2,1)} %bitcast.55, bf16[2,2,4,2,24,3072]{5,4,3,2,1,0:T(8,128)(2,1)} %bitcast.52, bf16[2,2,4,2,96,768]{5,4,3,2,1,0:T(8,128)(2,1)} %bitcast.53, f32[8,768]{1,0:T(8,128)} %get-tuple-element.107.refs_3_, bf16[192,768]{1,0:T(8,128)(2,1)} %get-tuple-element.108.refs_4_, ...), custom_call_target="tpu_custom_call" | custom-call | tf_op jit(solution)/shard_map/pallas_call | solution.py:1033
  396.9 1.8 copy-done
  398.8 1.6 shard_map.393
  400.3 0.6 slice_reduce_fusion.4
  401.0 0.7 slice_reduce_fusion
  (27 shorter events, 0.1 us)
Async XLA Ops:
  180.7 6.0 %slice-start.2 = ((s8[4718592]{0:T(1024)(128)(4,1)}), s8[4194304]{0:T(1024)(128)(4,1)S(1)}, s32[]{:S(2)}) async-start(s8[4718592]{0:T(1024)(128)(4,1)} %bitcast.63), calls=%async_computation.2 | async-start | bytes 8388608
  182.9 3.8 copy-start.4
  182.9 3.8 slice-start.3
  186.7 2.3 copy-start.7
  186.8 5.1 %slice-start = ((s8[4718592]{0:T(1024)(128)(4,1)}), s8[4194304]{0:T(1024)(128)(4,1)S(1)}, s32[]{:S(2)}) async-start(s8[4718592]{0:T(1024)(128)(4,1)} %bitcast.48), calls=%async_computation | async-start | bytes 8388608
  189.0 2.9 slice-start.1
  193.8 1.3 copy-start.6
  194.4 2.0 copy-start.8
  195.0 7.2 %copy-start.5 = (f32[192,768]{1,0:T(8,128)}, f32[192,768]{1,0:T(8,128)S(1)}, u32[]{:S(2)}) copy-start(f32[192,768]{1,0:T(8,128)S(1)} %fusion.12.refs_13_) | copy-start | bytes 1769476
  287.5 109.4 %copy-start.1 = (f32[24,3072]{1,0:T(8,128)S(1)}, f32[24,3072]{1,0:T(8,128)}, u32[]{:S(2)}) copy-start(f32[24,3072]{1,0:T(8,128)} %get-tuple-element.101.refs_0_) | copy-start | bytes 884740
  287.5 109.4 %copy-start.2 = (f32[96,768]{1,0:T(8,128)S(1)}, f32[96,768]{1,0:T(8,128)}, u32[]{:S(2)}) copy-start(f32[96,768]{1,0:T(8,128)} %get-tuple-element.102.refs_1_) | copy-start | bytes 884740
  287.5 109.4 %copy-start.3 = (f32[24,768]{1,0:T(8,128)S(1)}, f32[24,768]{1,0:T(8,128)}, u32[]{:S(2)}) copy-start(f32[24,768]{1,0:T(8,128)} %get-tuple-element.103.refs_2_) | copy-start | bytes 221188
  396.9 1.8 copy-start

commit v2 on v1

--- a/solution.py
+++ b/solution.py
@@ -19,8 +19,8 @@
 PLACES = (4, 5, 6, 7, 9)
 MIDDLE = (1, 1, 2, 3, 4, 5, 6, 7, 8)
 EARLY = 2
-RUNS = (8, 9, 9, 10, 11, 12)
-AHEAD = 5
+RUNS = (6, 9, 9, 10, 11, 12)
+AHEAD = 4
 F32 = jnp.float32
 BF16 = jnp.bfloat16
 
@@ -600,7 +600,7 @@
     gather.run(EARLY)
     kernel_rows(*[a[...].astype(F32) for a in states], cols, kernel_ref, blocks * rows)
     gather.run(RUNS[0])
-    gather.own_arrived(range(5))
+    gather.own_arrived(range(3))
     all_gains = gains[...].reshape(features, 128)
     normed_ref[...] = (standard_ref[...] * all_gains[:, :1]).astype(BF16)
 
@@ -612,8 +612,9 @@
     sent_kv[...] = wide[...].astype(BF16)
     over = Swap(sent_kv, came_kv, swap_sem.at[0], swap_sem.at[1])
     over.start()
+    gather.run(RUNS[1])
+    gather.own_arrived(range(3, 5))
     queries_ref[...] = projected(query_all)
-    gather.run(RUNS[1])
     over.wait()
     wide[...] = came_kv[...].astype(F32)
     for ch in range(channels):

time: 405 us -> 400 us (0.988)
  no operation moved by 1% of the time
where the time goes in v2:
time: 400 us; the launch traced here: 397 us
  Pallas kernels  364 us (91%)
  matrix products  21.6 us (5%)
  local copies, waits for them, and re-layouts  5.62 us (1%)
  other arithmetic  4.86 us (1%)
    pallas_call x1, Pallas kernels, first_layer(): pl.pallas_call(partial(first_body, parts, count), out_shape=[jax.ShapeDty...  172 us
    pallas_call x1, Pallas kernels, last_layer(): pl.pallas_call(partial(last_body, parts, count, kinds), out_shape=results...  108 us
    pallas_call x1, Pallas kernels, middle_layers(): pl.pallas_call(partial(middle_body, parts, count, kinds), out_shape=resul...  81.9 us
    dot_general x8, matrix products, contract(): lax.dot_general(left_side, right_side, (((left_dim,), (right_dim,)), ((),...  21.6 us

profile of v2, /device:TPU:0, one launch (start us, length us, event | category | flops | bytes accessed | tf_op | source)
XLA Modules:
  0.0 397.4 jit_solution(3329308613194624627)
XLA Ops:
  1.3 0.6 compare_convert_fusion.1.refs_12_.refs_6_
  1.9 0.7 stack.23
  2.6 0.6 compare_convert_fusion.refs_13_.refs_10_
  3.2 0.1 copy.55
  3.3 0.6 pad_convert_fusion.refs_0_.refs_14_.refs_23_
  3.9 171.7 %shard_map.390 = (f32[32,24,128]{2,1,0:T(8,128)}, bf16[32,24,768]{2,1,0:T(8,128)(2,1)}, bf16[32,24,768]{2,1,0:T(8,128)(2,1)}, bf16[32,24,768]{2,1,0:T(8,128)(2,1...) custom-call(f32[24,128]{1,0:T(8,128)} %pad_convert_fusion.refs_0_.re, ...), custom_call_target="tpu_custom_call" | custom-call | tf_op jit(solution)/shard_map/pallas_call | solution.py:735
  175.7 1.2 reduce_sum.43
  176.9 0.0 slice-start.2
  176.9 1.4 multiply_reduce_fusion.2
  178.3 0.8 slice_reduce_fusion.5
  179.1 0.0 copy-start.4
  179.1 0.0 slice-start.3
  179.1 3.7 fusion.25
  182.9 0.0 copy-start.7
  182.9 0.0 slice-start
  182.9 2.2 fusion.9
  185.1 2.9 fusion.6
  188.0 1.9 multiply_reduce_fusion
  189.9 0.6 reshape.133.refs_19_
  190.5 0.3 fusion.26
  190.8 0.2 fusion.12.refs_13_
  191.0 0.2 copy-done.6
  191.2 1.3 convolution_convert_fusion.3.refs_9_
  192.5 1.6 convolution_convert_fusion.2
  194.0 4.3 %convolution_convert_fusion = bf16[3072,768]{1,0:T(8,128)(2,1)} fusion(bf16[1,192,768]{2,1,0:T(8,128)(2,1)S(1)} %copy-done.7, f32[192]{0:T(256)S(1)} %compare_convert_fusion.2, f32[192,3072]{1,0:T(8,128)S(1)} %fusion.25), kind=kOutput, calls=%fused_computation | convolution fusion | flops 914079744 | bytes 7373568 | tf_op jit(solution)/shard_map/dot_general | solution.py:364
  198.3 3.7 convolution_convert_fusion.1
  202.0 81.9 %shard_map.391 = (f32[24,3072]{1,0:T(8,128)}, f32[96,768]{1,0:T(8,128)}, f32[24,768]{1,0:T(8,128)}, bf16[32,24,2304]{2,1,0:T(8,128)(2,1)}, bf16[32,24,3072]{2,1,...) custom-call(bf16[2,2,4,2,24,3072]{5,4,3,2,1,0:T(8,128)(2,1)} %bitcas, ...), custom_call_target="tpu_custom_call" | custom-call | tf_op jit(solution)/shard_map/pallas_call | solution.py:1328
  284.0 108.4 %shard_map.392.refs_3_ = f32[240,3072]{1,0:T(8,128)} custom-call(bf16[2,2,4,2,24,2304]{5,4,3,2,1,0:T(8,128)(2,1)} %bitcast.55, bf16[2,2,4,2,24,3072]{5,4,3,2,1,0:T(8,128)(2,1)} %bitcast.52, bf16[2,2,4,2,96,768]{5,4,3,2,1,0:T(8,128)(2,1)} %bitcast.53, f32[8,768]{1,0:T(8,128)} %get-tuple-element.107.refs_3_, bf16[192,768]{1,0:T(8,128)(2,1)} %get-tuple-element.108.refs_4_, ...), custom_call_target="tpu_custom_call" | custom-call | tf_op jit(solution)/shard_map/pallas_call | solution.py:1034
  392.4 1.8 copy-done
  394.2 1.6 shard_map.393
  395.8 0.6 slice_reduce_fusion.4
  396.5 0.7 slice_reduce_fusion
  (27 shorter events, 0.1 us)
Async XLA Ops:
  176.9 6.0 %slice-start.2 = ((s8[4718592]{0:T(1024)(128)(4,1)}), s8[4194304]{0:T(1024)(128)(4,1)S(1)}, s32[]{:S(2)}) async-start(s8[4718592]{0:T(1024)(128)(4,1)} %bitcast.63), calls=%async_computation.2 | async-start | bytes 8388608
  179.1 3.8 copy-start.4
  179.1 3.8 slice-start.3
  182.9 2.3 copy-start.7
  182.9 5.1 %slice-start = ((s8[4718592]{0:T(1024)(128)(4,1)}), s8[4194304]{0:T(1024)(128)(4,1)S(1)}, s32[]{:S(2)}) async-start(s8[4718592]{0:T(1024)(128)(4,1)} %bitcast.48), calls=%async_computation | async-start | bytes 8388608
  185.1 2.9 slice-start.1
  189.9 1.3 copy-start.6
  190.5 1.9 copy-start.8
  191.2 7.2 %copy-start.5 = (f32[192,768]{1,0:T(8,128)}, f32[192,768]{1,0:T(8,128)S(1)}, u32[]{:S(2)}) copy-start(f32[192,768]{1,0:T(8,128)S(1)} %fusion.12.refs_13_) | copy-start | bytes 1769476
  284.0 108.4 %copy-start.1 = (f32[24,3072]{1,0:T(8,128)S(1)}, f32[24,3072]{1,0:T(8,128)}, u32[]{:S(2)}) copy-start(f32[24,3072]{1,0:T(8,128)} %get-tuple-element.101.refs_0_) | copy-start | bytes 884740
  284.0 108.4 %copy-start.2 = (f32[96,768]{1,0:T(8,128)S(1)}, f32[96,768]{1,0:T(8,128)}, u32[]{:S(2)}) copy-start(f32[96,768]{1,0:T(8,128)} %get-tuple-element.102.refs_1_) | copy-start | bytes 884740
  284.0 108.4 %copy-start.3 = (f32[24,768]{1,0:T(8,128)S(1)}, f32[24,768]{1,0:T(8,128)}, u32[]{:S(2)}) copy-start(f32[24,768]{1,0:T(8,128)} %get-tuple-element.103.refs_2_) | copy-start | bytes 221188
  392.4 1.8 copy-start
